TPU v7x, 128 devices: a whole 4x4x4 slice. The times are simulated.
128 devices in a mesh: param: 32 (over z, y, core), ex: 4 (over x).
Axes of the slice: x: 4, y: 4, z: 4, core: 2. Of those that a mesh axis runs over, the one named last changes fastest.
Arguments:
- inputs: bfloat16 [16, 128, 4096], P('ex', None, 'param'), may hold values from -6 to 6
- cotangents: bfloat16 [3, 16, 128, 4096], P(None, 'ex', None, 'param'), may hold values from -6 to 6
- jl_bank: bfloat16 [64, 128, 128], replicated, may hold values from -0.5 to 0.5
- jl_tiles: int32 [3, 32, 32, 8], replicated, may hold values from 0 to 63
- jl_blocks: int32 [3, 32, 32, 8], replicated, may hold values from 0 to 31
- jl_signs: int32 [3, 32, 32, 8], replicated, may hold values from 0 to 1
- test_features: bfloat16 [1024, 4096], P('ex', 'param'), may hold values from -6 to 6
Outputs:
- scores: float32 [16, 1024], P('ex')
All inputs are finite; a program needn't handle non-finite values.
Results may differ from a plain program's by a relative error of at most 0.007.
Values may be sent and summed in bfloat16 or wider, within the bound.
A program may use at most 64 MiB of HBM per device.

v0:
```python
import math

import jax
import jax.numpy as jnp
from jax import lax
from jax.sharding import PartitionSpec as P

D = 4096
K = 4096
TILE = 128
HITS = 8
MATS = 3
TOK = 128


def tile_terms(in_tiles, out_tiles, row_first, col_first, jl_bank, jl_tiles, jl_blocks, jl_signs):
    mat_count = out_tiles.shape[0]
    row_count = in_tiles.shape[2]
    col_count = out_tiles.shape[3]
    hit_count = jl_tiles.shape[3]
    corner = (0, row_first, col_first, 0)
    extent = (mat_count, row_count, col_count, hit_count)
    tile_ids = lax.dynamic_slice(jl_tiles, corner, extent)
    block_ids = lax.dynamic_slice(jl_blocks, corner, extent)
    sign_bits = lax.dynamic_slice(jl_signs, corner, extent)
    bank_tiles = jnp.take(jl_bank, tile_ids, axis=0)
    products = jnp.einsum(
        "metjk,mijhka->metijha", out_tiles, bank_tiles, preferred_element_type=jnp.float32
    ).astype(jnp.bfloat16)
    weighted = jnp.einsum(
        "metijha,etia->meijha", products, in_tiles, preferred_element_type=jnp.float32
    )
    select = (block_ids[..., None] == jnp.arange(K // TILE, dtype=jnp.int32)).astype(jnp.float32)
    select = select * (2 * sign_bits - 1).astype(jnp.float32)[..., None]
    return jnp.einsum("meijha,mijhb->eba", weighted, select, precision=lax.Precision.HIGHEST)


def local(inputs, cotangents, jl_bank, jl_tiles, jl_blocks, jl_signs, test_features):
    examples = inputs.shape[0]
    zero_sums = jnp.zeros((examples, K // TILE, TILE), jnp.float32)
    row_count = inputs.shape[2] // TILE
    row_first = lax.axis_index("param") * row_count
    in_tiles = inputs.reshape(examples, TOK, row_count, TILE)
    segment = lax.all_gather(cotangents, "param", axis=3, tiled=True)
    col_count = segment.shape[3] // TILE
    col_tiles = segment.reshape(segment.shape[0], examples, TOK, col_count, TILE)

    def add_column(column, carried):
        out_tiles = lax.dynamic_slice_in_dim(col_tiles, column, 1, 3)
        return carried + tile_terms(
            in_tiles, out_tiles, row_first, column, jl_bank, jl_tiles, jl_blocks, jl_signs
        )

    partial_sums = lax.fori_loop(0, col_count, add_column, zero_sums)
    owned_blocks = lax.psum_scatter(partial_sums, "param", scatter_dimension=1, tiled=True)
    features = owned_blocks.reshape(examples, -1) / math.sqrt(
        TOK * MATS * HITS * D * D / (TILE * K)
    )
    partial_scores = jnp.dot(
        features,
        lax.all_gather(test_features, "ex", axis=0, tiled=True).astype(jnp.float32).T,
        precision=lax.Precision.HIGHEST,
    )
    return lax.psum(partial_scores, "param") / math.sqrt(K)


def solution(mesh):
    placed = (
        P("ex", None, "param"),
        P(None, "ex", None, "param"),
        P(),
        P(),
        P(),
        P(),
        P("ex", "param"),
    )
    return jax.shard_map(
        local, mesh=mesh, in_specs=placed, out_specs=P("ex", None), check_vma=False
    )
```

profile of v0, /device:TPU:1, one launch (start us, length us, event | category | flops | bytes accessed | tf_op | source)
XLA Modules:
  0.0 548.6 jit_solution(6337774161395588356)
XLA Ops:
  14.9 61.4 %all-gather.2.cloned.1.call-done = bf16[3,4,128,4096]{2,3,1,0:T(8,128)(2,1)} async-done(((bf16[3,4,128,128]{2,3,1,0:T(8,128)(2,1)}), bf16[3,4,128,4096]{2,3,1,0:T(8,128)(2,1)}) %all-gather.2.cloned.1.call-update) | async-done | bytes 12582928 | tf_op jit(solution)/shard_map/all_gather | solution.py:44
  76.3 247.7 %while.16 = (s32[]{:T(128)}, f32[4,32,128]{2,1,0:T(8,128)S(1)}, s32[3,32,32,8]{3,0,2,1:T(4,128)}, s32[]{:T(128)}, s32[3,32,32,8]{3,0,2,1:T(4,128)}, /*index=5*/s...) while((s32[]{:T(128)}, f32[4,32,128]{2,1,0:T(8,128)S(1)}, ...), condition=%wide.region_1.0_spmd.clone, body=%wide.region_0.1_spmd.clone.sunk | while | flops 414145248 | bytes 5740343 | solution.py:54
  80.0 3.0 multiply_reduce_fusion.2
  103.2 3.0 multiply_reduce_fusion.2
  111.0 3.0 multiply_reduce_fusion.2
  118.7 3.0 multiply_reduce_fusion.2
  126.5 3.0 multiply_reduce_fusion.2
  134.2 3.0 multiply_reduce_fusion.2
  149.7 3.0 multiply_reduce_fusion.2
  165.2 3.0 multiply_reduce_fusion.2
  172.9 3.0 multiply_reduce_fusion.2
  180.6 3.0 multiply_reduce_fusion.2
  188.4 3.0 multiply_reduce_fusion.2
  196.2 3.0 multiply_reduce_fusion.2
  203.9 3.0 multiply_reduce_fusion.2
  211.6 3.0 multiply_reduce_fusion.2
  219.4 3.0 multiply_reduce_fusion.2
  227.1 3.0 multiply_reduce_fusion.2
  234.8 3.0 multiply_reduce_fusion.2
  242.6 3.0 multiply_reduce_fusion.2
  250.3 3.0 multiply_reduce_fusion.2
  258.1 3.0 multiply_reduce_fusion.2
  265.8 3.0 multiply_reduce_fusion.2
  273.5 3.0 multiply_reduce_fusion.2
  281.3 3.0 multiply_reduce_fusion.2
  289.0 3.0 multiply_reduce_fusion.2
  304.5 3.0 multiply_reduce_fusion.2
  312.2 3.0 multiply_reduce_fusion.2
  320.0 3.0 multiply_reduce_fusion.2
  324.7 10.3 %all_gather.7 = bf16[1024,128]{1,0:T(8,128)(2,1)S(1)} all-gather(bf16[256,128]{1,0:T(8,128)(2,1)S(1)} %copy-done.3), channel_id=1, replica_groups=mesh['param'=32,'ex'=4] {'ex'}, dimensions={0}, use_global_device_ids=true | all-gather | bytes 327680 | tf_op jit(solution)/shard_map/all_gather | solution.py:61
  335.6 84.0 %all-reduce.3.cloned.1.call-done = f32[4,32,128]{2,0,1:T(4,128)} async-done(((f32[4,32,128]{2,0,1:T(4,128)}), f32[4,32,128]{2,0,1:T(4,128)}) %all-reduce.3.cloned.1.call-update) | async-done | bytes 65552
  421.2 120.0 %psum.7 = f32[4,1024]{1,0:T(4,128)S(1)} all-reduce(f32[4,1024]{1,0:T(4,128)S(1)} %fusion.18), channel_id=1, replica_groups=mesh['param'=32,'ex'=4] {'param'}, use_global_device_ids=true, to_apply=%region_3.4 | all-reduce | flops 4096 | bytes 32768 | tf_op jit(solution)/shard_map/psum | solution.py:64
  (316 shorter events, 176.9 us)
Async XLA Ops:
  6.5 4.8 copy-start.1
  6.5 6.6 %copy-start.2 = (s32[3,32,32,8]{2,3,1,0:T(8,128)S(1)}, s32[3,32,32,8]{2,3,1,0:T(8,128)}, u32[]{:S(2)}) copy-start(s32[3,32,32,8]{2,3,1,0:T(8,128)} %param.12) | copy-start | bytes 294916
  6.5 69.8 %all-gather.2.cloned.1.call-start = ((), (), s32[]{:S(2)}) async-start(), calls=%async_computation | async-start | bytes 12976128 | tf_op jit(solution)/shard_map/all_gather | solution.py:44
  8.5 411.0 %all-reduce.3.cloned.1.call-start = ((), (), s32[]{:S(2)}) async-start(), calls=%async_computation.1 | async-start | bytes 131072
  8.6 67.7 %copy-start = (bf16[4,128,128]{2,1,0:T(8,128)(2,1)S(1)}, bf16[4,128,128]{2,1,0:T(8,128)(2,1)}, u32[]{:S(2)}) copy-start(bf16[4,128,128]{2,1,0:T(8,128)(2,1)} %param.9) | copy-start | bytes 393220
  76.3 248.4 %copy-start.3 = (bf16[256,128]{1,0:T(8,128)(2,1)S(1)}, bf16[256,128]{1,0:T(8,128)(2,1)}, u32[]{:S(2)}) copy-start(bf16[256,128]{1,0:T(8,128)(2,1)} %param.15) | copy-start | bytes 196612
  76.3 258.7 %copy-start.4 = (u32[128]{0:T(128)S(1)}, u32[128]{0:T(128)}, u32[]{:S(2)}) copy-start(u32[128]{0:T(128)} %constant.114) | copy-start | bytes 1540
Sparse Core Ops, SparseCore 0:
  9.7 66.5 all-gather.1
  324.8 94.6 all-reduce.2
where the time goes:
time: 557 us; the launch traced here: 549 us
  waiting for transfers between devices  145 us (26%)
  blocking collectives  130 us (23%)
  matrix products  108 us (19%)
  local copies, waits for them, and re-layouts  104 us (19%)
  other arithmetic  45.8 us (8%)
  between operations  13.4 us (2%)
    psum x1, blocking collectives, local(): return lax.psum(partial_scores, 'param') / math.sqrt(K)  120 us
    dot_general x32, matrix products, tile_terms(): jnp.einsum('metjk,mijhka->metijha', out_tiles, bank_tiles, preferred_elem...  95.6 us
    gather x64, local copies, waits for them, and re-layouts, tile_terms(): bank_tiles = jnp.take(jl_bank, tile_ids, axis=0)  87.9 us
    unnamed x3, waiting for transfers between devices  84 us
    all_gather x1, waiting for transfers between devices, local(): segment = lax.all_gather(cotangents, 'param', axis=3, tiled=True)  61.4 us
    mul x32, other arithmetic, tile_terms(): select = select * (2 * sign_bits - 1).astype(jnp.float32)[..., None]  22.2 us
    reduce_and x32, other arithmetic, tile_terms(): bank_tiles = jnp.take(jl_bank, tile_ids, axis=0)  22 us
  transfers between devices with their start and end apart: 2, of which 2 were waited for; matrix products, arithmetic and copies ran while one was open for 1% of the time, Pallas kernels for 0%

commit v1 on v0

v1 whole, which is shorter than its diff:
```python
import functools
import math

import jax
import jax.numpy as jnp
from jax import lax
from jax.experimental import pallas as pl
from jax.experimental.pallas import tpu as pltpu
from jax.sharding import PartitionSpec as P

D = 4096
K = 4096
TILE = 128
HITS = 8
MATS = 3
TOK = 128
BANK = 64
BLOCKS = 32
EX = 4
ROWS = 8
COLS = 4
PAIRS = MATS * COLS // 2
GROUP = 32
BATCH = 2
MESH = pl.DeviceIdType.MESH
F32 = jnp.float32
BF16 = jnp.bfloat16
SCALE = 1.0 / (math.sqrt(TOK * MATS * HITS * D * D / (TILE * K)) * math.sqrt(K))
ORDER = (0, 2, 1, 3)


def dot(a, b):
    return lax.dot_general(a, b, (((1,), (0,)), ((), ())), preferred_element_type=F32)


def dot_nt(a, b):
    return lax.dot_general(a, b, (((1,), (1,)), ((), ())), preferred_element_type=F32)


def kernel(
    in_hbm, cot_hbm, bank_hbm, tiles_hbm, blocks_hbm, signs_hbm, test_hbm, out_ref,
    bank, bank_t, hits, cots, ins, left32, left, grads, quads, picked, count, tests,
    raw, raw_in, part, part_in, done,
    load_sem, own_sem, j_send, j_recv, i_send, i_recv, t_send, t_recv, ex_send, ex_recv,
):
    me = lax.axis_index("param")
    mx = lax.axis_index("ex")
    core = lax.rem(me, 2)
    y = lax.rem(me // 2, 4)
    z = me // 8

    def device(zz, yy, cc):
        return (zz * 4 + yy) * 2 + cc

    loads = [
        pltpu.make_async_copy(tiles_hbm, hits.at[0], load_sem.at[0]),
        pltpu.make_async_copy(blocks_hbm, hits.at[1], load_sem.at[1]),
        pltpu.make_async_copy(signs_hbm, hits.at[2], load_sem.at[2]),
        pltpu.make_async_copy(bank_hbm, bank, load_sem.at[3]),
        pltpu.make_async_copy(test_hbm, tests.at[mx], load_sem.at[4]),
    ]
    for copy in loads:
        copy.start()
    row_slot = [z * 2 + core, z * 2 + core, y * 2 + core, y * 2 + core]
    col_slot = [y, y, z, z]
    own = []
    for e in range(EX):
        own.append(pltpu.make_async_copy(in_hbm.at[e], ins.at[e, row_slot[e]], own_sem.at[e, 0]))
        own.append(pltpu.make_async_copy(cot_hbm.at[:, e], cots.at[e, col_slot[e]], own_sem.at[e, 1]))
    for copy in own:
        copy.start()

    barrier = pltpu.get_barrier_semaphore()

    def greet(d, carry):
        pl.semaphore_signal(
            barrier, inc=1, device_id={"param": lax.rem(me + d, GROUP)}, device_id_type=MESH
        )
        return carry

    lax.fori_loop(1, GROUP, greet, 0)
    for d in range(1, 4):
        pl.semaphore_signal(barrier, inc=1, device_id={"ex": lax.rem(mx + d, 4)}, device_id_type=MESH)
    pl.semaphore_wait(barrier, GROUP - 1 + 3)

    col_copies, row_copies = {}, {}
    for e in ORDER:
        along_y = e < 2
        for d in (1, 3, 2):
            if along_y:
                to = device(z, lax.rem(y + d, 4), core)
            else:
                to = device(lax.rem(z + d, 4), y, core)
            col_copies[e, d] = pltpu.make_async_remote_copy(
                src_ref=cot_hbm.at[:, e],
                dst_ref=cots.at[e, col_slot[e]],
                send_sem=j_send.at[e, d - 1],
                recv_sem=j_recv.at[e, d - 1],
                device_id={"param": to},
                device_id_type=MESH,
            )
            col_copies[e, d].start()
        for d in (1, 2, 3, 6, 7, 4, 5):
            other = lax.rem(core + d, 2)
            if along_y:
                to = device(lax.rem(z + d // 2, 4), y, other)
            else:
                to = device(z, lax.rem(y + d // 2, 4), other)
            row_copies[e, d] = pltpu.make_async_remote_copy(
                src_ref=in_hbm.at[e],
                dst_ref=ins.at[e, row_slot[e]],
                send_sem=i_send.at[e, d - 1],
                recv_sem=i_recv.at[e, d - 1],
                device_id={"param": to},
                device_id_type=MESH,
            )
            row_copies[e, d].start()
    test_copies = []
    for d in range(1, 4):
        copy = pltpu.make_async_remote_copy(
            src_ref=test_hbm,
            dst_ref=tests.at[mx],
            send_sem=t_send.at[d - 1],
            recv_sem=t_recv.at[d - 1],
            device_id={"ex": lax.rem(mx + d, 4)},
            device_id_type=MESH,
        )
        copy.start()
        test_copies.append(copy)

    for copy in loads:
        copy.wait()
    lane = lax.broadcasted_iota(jnp.int32, (HITS, TILE), 1)
    block_of_lane = lax.rem(lane, BLOCKS).astype(F32)
    quarter = lane // BLOCKS
    tile_of_row = lax.broadcasted_iota(jnp.int32, (BANK, 2 * TILE), 0).astype(F32)
    for kind in range(2):
        first, step = (z * 8 + core, 2) if kind == 0 else (y * 2 + core, 8)
        source = lax.broadcasted_iota(jnp.int32, (GROUP, COLS * TILE), 0)
        column = lax.broadcasted_iota(jnp.int32, (GROUP, COLS * TILE), 1) // TILE
        choose = jnp.where(source == first + step * column, 1.0, 0.0).astype(BF16)
        for m in range(MATS):
            spread = []
            for which in range(3):
                if kind == 0:
                    rows = [
                        hits[which, m, pl.ds(zz * 8 + y * 2, 2)].reshape(2 * HITS, GROUP)
                        for zz in range(4)
                    ]
                    values = jnp.concatenate(rows, axis=0)
                else:
                    values = hits[which, m, pl.ds(z * 8, ROWS)].reshape(ROWS * HITS, GROUP)
                spread.append(dot(values.astype(F32).astype(BF16), choose))

            def lanes_of(values, col, half):
                parts = [
                    values[(half * 4 + q) * HITS : (half * 4 + q + 1) * HITS, col * TILE : (col + 1) * TILE]
                    for q in range(4)
                ]
                low = jnp.where(quarter == 0, parts[0], parts[1])
                high = jnp.where(quarter == 2, parts[2], parts[3])
                return jnp.where(quarter < 2, low, high)

            for col in range(COLS):
                tile_rows, sign_rows = [], []
                for half in range(2):
                    tile, block, sign = [lanes_of(values, col, half) for values in spread]
                    tile_rows.append(jnp.where(block == block_of_lane, tile, -1.0))
                    sign_rows.append(2.0 * sign - 1.0)
                tile_rows = jnp.concatenate(tile_rows, axis=1)
                sign_rows = jnp.concatenate(sign_rows, axis=1)
                total = jnp.zeros((BANK, 2 * TILE), F32)
                for h in range(HITS):
                    total += jnp.where(
                        tile_of_row == tile_rows[h : h + 1, :], sign_rows[h : h + 1, :], 0.0
                    )
                at = (m * COLS + col) * BANK
                count[kind, at : at + BANK, :] = total.astype(BF16)

    def turn(r, carry):
        bank_t[pl.ds(r, TILE, stride=BANK), :] = bank[r].astype(F32).T
        return carry

    lax.fori_loop(0, BANK, turn, 0, unroll=4)
    for copy in own:
        copy.wait()

    raw[...] = jnp.zeros_like(raw)
    row_in_group = lax.rem(lax.broadcasted_iota(jnp.int32, (256, TILE), 0), ROWS)
    lane_group = lax.broadcasted_iota(jnp.int32, (256, TILE), 1) // BLOCKS
    upper = row_in_group >= 4
    keep = lane_group == lax.rem(row_in_group, 4)

    for first in range(0, EX, BATCH):
        batch = ORDER[first : first + BATCH]
        for slot, e in enumerate(batch):
            for d in range(1, 8):
                row_copies[e, d].wait_recv()

            def turn_rows(i, carry, e=e):
                left32[pl.ds(i, TILE, stride=ROWS), :] = ins[e, i].astype(F32).T
                return carry

            lax.fori_loop(0, ROWS, turn_rows, 0, unroll=4)
            left[...] = left32[...].astype(BF16)
            for d in range(1, 4):
                col_copies[e, d].wait_recv()

            def gradient(pair, carry, e=e, slot=slot):
                m = pair // 2
                col = lax.rem(pair, 2) * 2
                right = jnp.concatenate([cots[e, col, m], cots[e, col + 1, m]], axis=1)
                grads[slot, pair] = dot(left[...], right)
                return carry

            lax.fori_loop(0, PAIRS, gradient, 0)

        def project(a, carry):
            at = pl.multiple_of(a * ROWS, ROWS)
            lhs = jnp.concatenate(
                [grads[slot, pair, pl.ds(at, ROWS), :] for slot in range(BATCH) for pair in range(PAIRS)],
                axis=0,
            ).astype(BF16)
            tiles = bank_t[pl.ds(pl.multiple_of(a * BANK, BANK), BANK), :].astype(BF16)
            zero = jnp.zeros_like(tiles)
            weights = jnp.concatenate(
                [jnp.concatenate([tiles, zero], axis=1), jnp.concatenate([zero, tiles], axis=1)], axis=0
            )
            out = dot_nt(lhs, weights)
            for slot in range(BATCH):
                for pair in range(PAIRS):
                    src = (slot * PAIRS + pair) * ROWS
                    quads[slot, pl.ds(at, ROWS), pair * TILE : (pair + 1) * TILE] = out[src : src + ROWS]
            return carry

        lax.fori_loop(0, TILE, project, 0, unroll=4)

        for slot, e in enumerate(batch):
            kind = 0 if e < 2 else 1

            def select(chunk, carry, slot=slot, kind=kind):
                at = pl.multiple_of(chunk * 256, 256)
                sums = dot(quads[slot, pl.ds(at, 256), :].astype(BF16), count[kind])
                folded = jnp.where(upper, sums[:, TILE:], sums[:, :TILE])
                picked[pl.ds(at, 256), :] = jnp.where(keep, folded, 0.0)
                return carry

            lax.fori_loop(0, TILE * ROWS // 256, select, 0)
            total = picked[pl.ds(0, TILE, stride=ROWS), :]
            for i in range(1, ROWS):
                total += picked[pl.ds(i, TILE, stride=ROWS), :]
            turned = total.T
            folded = turned[0:32] + turned[32:64] + turned[64:96] + turned[96:128]
            raw[pl.ds(e, BLOCKS, stride=8), :] = folded

    def exchange(index, source, target):
        def copy(d):
            return pltpu.make_async_remote_copy(
                src_ref=source(lax.rem(me + d, GROUP)),
                dst_ref=target,
                send_sem=ex_send.at[index, d],
                recv_sem=ex_recv.at[index, d],
                device_id={"param": lax.rem(me + d, GROUP)},
                device_id_type=MESH,
            )

        def start(d, carry):
            copy(d).start()
            return carry

        def wait(d, carry):
            copy(d).wait_recv()
            return carry

        def drain(d, carry):
            copy(d).wait_send()
            return carry

        lax.fori_loop(1, GROUP, start, 0)
        lax.fori_loop(1, GROUP, wait, 0)
        return lambda: lax.fori_loop(1, GROUP, drain, 0)

    raw_in[me] = raw[pl.ds(pl.multiple_of(me * 8, 8), 8), :]
    drains = [
        exchange(0, lambda to: raw.at[pl.ds(pl.multiple_of(to * 8, 8), 8), :], raw_in.at[me])
    ]
    features = jnp.sum(raw_in[...], axis=0) * SCALE
    high = features.astype(BF16)
    low = (features - high.astype(F32)).astype(BF16)
    both = jnp.concatenate([high, low], axis=0)
    for copy in test_copies:
        copy.wait_recv()
    for quarter_of in range(4):
        scores = dot_nt(both, tests[quarter_of])
        scores = scores[:8] + scores[8:]
        for half in range(2):
            for e in range(EX):
                part[(quarter_of * 2 + half) * EX + e] = scores[e : e + 1, half * TILE : (half + 1) * TILE]
    part_in[me] = part[me]
    drains.append(exchange(1, lambda to: part.at[to], part_in.at[me]))
    done[me] = jnp.sum(part_in[...], axis=0)
    drains.append(exchange(2, lambda to: done.at[me], done.at[me]))
    for chunk in range(8):
        for e in range(EX):
            out_ref[e : e + 1, chunk * TILE : (chunk + 1) * TILE] = done[chunk * EX + e]
    for drain in drains:
        drain()
    for copy in list(col_copies.values()) + list(row_copies.values()) + test_copies:
        copy.wait_send()


def local(inputs, cotangents, jl_bank, jl_tiles, jl_blocks, jl_signs, test_features):
    turned = [jnp.transpose(a, (0, 1, 3, 2)) for a in (jl_tiles, jl_blocks, jl_signs)]
    anywhere = pl.BlockSpec(memory_space=pl.ANY)
    dma = pltpu.SemaphoreType.DMA
    return pl.pallas_call(
        kernel,
        out_shape=jax.ShapeDtypeStruct((EX, 1024), F32),
        in_specs=[anywhere] * 7,
        out_specs=pl.BlockSpec(memory_space=pltpu.VMEM),
        scratch_shapes=[
            pltpu.VMEM((BANK, TILE, TILE), BF16),
            pltpu.VMEM((TILE * BANK, TILE), F32),
            pltpu.VMEM((3, MATS, GROUP, HITS, GROUP), jnp.int32),
            pltpu.VMEM((EX, COLS, MATS, TOK, TILE), BF16),
            pltpu.VMEM((EX, ROWS, TOK, TILE), BF16),
            pltpu.VMEM((TILE * ROWS, TOK), F32),
            pltpu.VMEM((TILE * ROWS, TOK), BF16),
            pltpu.VMEM((BATCH, PAIRS, TILE * ROWS, 2 * TILE), F32),
            pltpu.VMEM((BATCH, TILE * ROWS, PAIRS * TILE), F32),
            pltpu.VMEM((TILE * ROWS, TILE), F32),
            pltpu.VMEM((2, MATS * COLS * BANK, 2 * TILE), BF16),
            pltpu.VMEM((4, 256, TILE), BF16),
            pltpu.VMEM((BLOCKS * 8, TILE), F32),
            pltpu.VMEM((GROUP, 8, TILE), F32),
            pltpu.VMEM((GROUP, 1, TILE), F32),
            pltpu.VMEM((GROUP, 1, TILE), F32),
            pltpu.VMEM((GROUP, 1, TILE), F32),
            dma((5,)),
            dma((EX, 2)),
            dma((EX, 3)),
            dma((EX, 3)),
            dma((EX, 7)),
            dma((EX, 7)),
            dma((3,)),
            dma((3,)),
            dma((3, GROUP)),
            dma((3, GROUP)),
        ],
        compiler_params=pltpu.CompilerParams(
            collective_id=0, has_side_effects=True, vmem_limit_bytes=56 * 1024 * 1024
        ),
        cost_estimate=pl.CostEstimate(flops=9_000_000_000, bytes_accessed=8_000_000, transcendentals=0),
    )(inputs, cotangents, jl_bank, *turned, test_features)


def solution(mesh):
    placed = (
        P("ex", None, "param"),
        P(None, "ex", None, "param"),
        P(),
        P(),
        P(),
        P(),
        P("ex", "param"),
    )
    return jax.shard_map(
        local, mesh=mesh, in_specs=placed, out_specs=P("ex", None), check_vma=False
    )
```

time: 557 us -> 63.5 us (0.11); the launches traced: 549 us -> 63.3 us
  waiting for transfers between devices: 145 us -> 0 us
  blocking collectives: 130 us -> 0 us
  matrix products: 108 us -> 0 us
  local copies, waits for them, and re-layouts: 104 us -> 1.32 us
  Pallas kernels: 0 us -> 62 us
  other arithmetic: 45.8 us -> 0 us
  between operations: 13.4 us -> 0.01 us
    psum x1 -> x0, blocking collectives: 120 us -> none  [local(): return lax.psum(partial_scores, 'param') / math.sqrt(K)]
    dot_general x65 -> x0, matrix products: 108 us -> none  [the longest x32 95.6 us: tile_terms(): jnp.einsum('metjk,mijhka->metijha', out_tiles, bank_tiles, preferred_elem...]
    gather x64 -> x0, local copies, waits for them, and re-layouts: 87.9 us -> none  [tile_terms(): bank_tiles = jnp.take(jl_bank, tile_ids, axis=0)]
    unnamed x3 -> x0, waiting for transfers between devices: 84 us -> none
    pallas_call x0 -> x1, Pallas kernels: none -> 62 us  [local(): pl.pallas_call(kernel, out_shape=jax.ShapeDtypeStruct((EX, 1024), F32), i...]
    all_gather x1 -> x0, waiting for transfers between devices: 61.4 us -> none  [local(): segment = lax.all_gather(cotangents, 'param', axis=3, tiled=True)]
    mul x32 -> x0, other arithmetic: 22.2 us -> none  [tile_terms(): select = select * (2 * sign_bits - 1).astype(jnp.float32)[..., None]]
    reduce_and x32 -> x0, other arithmetic: 22 us -> none  [tile_terms(): bank_tiles = jnp.take(jl_bank, tile_ids, axis=0)]
  transfers between devices with their start and end apart: 2 -> 0, of which waited for: 2 -> 0; matrix products, arithmetic and copies ran while one was open for 1% -> 0% of each run, Pallas kernels for 0% -> 0%
where the time goes in v1:
time: 63.5 us; the launch traced here: 63.3 us
  Pallas kernels  62 us (98%)
  local copies, waits for them, and re-layouts  1.32 us (2%)
    pallas_call x1, Pallas kernels, local(): pl.pallas_call(kernel, out_shape=jax.ShapeDtypeStruct((EX, 1024), F32), i...  62 us
    unnamed x1, local copies, waits for them, and re-layouts  1.32 us

profile of v1, /device:TPU:1, one launch (start us, length us, event | category | flops | bytes accessed | tf_op | source)
XLA Modules:
  0.0 63.3 jit_solution(6559105952552012837)
XLA Ops:
  0.0 62.0 %shard_map.73 = f32[4,1024]{1,0:T(4,128)} custom-call(bf16[4,128,128]{2,1,0:T(8,128)(2,1)} %in_hbm.1, bf16[3,4,128,128]{3,2,1,0:T(8,128)(2,1)} %cot_hbm.1, bf16[64,128,128]{2,1,0:T(8,128)(2,1)} %bank_hbm.1, s32[3,32,8,32]{3,2,1,0:T(8,128)} %bitcast.3, s32[3,32,8,32]{3,2,1,0:T(8,128)} %bitcast.4, s32[3,32,8,32]{3,2,1,0:T(8,128)} %bitcast.5, ...), custom_call_target="tpu_custom_call" | custom-call | flops 8999999488 | bytes 8000000 | tf_op jit(solution)/shard_map/pallas_call | solution.py:316
  62.0 1.3 %copy.9 = f32[4,1024]{1,0:T(4,128)} copy(f32[4,1024]{1,0:T(4,128)} %shard_map.73) | data formatting | bytes 32768

commit v2 on v1

v2 whole, which is shorter than its diff:
```python
import functools
import math

import jax
import jax.numpy as jnp
from jax import lax
from jax.experimental import pallas as pl
from jax.experimental.pallas import tpu as pltpu
from jax.sharding import PartitionSpec as P

D = 4096
K = 4096
TILE = 128
HITS = 8
MATS = 3
TOK = 128
BANK = 64
BLOCKS = 32
EX = 4
ROWS = 8
COLS = 4
PAIRS = MATS * COLS // 2
GROUP = 32
MESH = pl.DeviceIdType.MESH
F32 = jnp.float32
BF16 = jnp.bfloat16
SCALE = 1.0 / (math.sqrt(TOK * MATS * HITS * D * D / (TILE * K)) * math.sqrt(K))
ORDER = (0, 2, 1, 3)


def dot(a, b):
    return lax.dot_general(a, b, (((1,), (0,)), ((), ())), preferred_element_type=F32)


def dot_nt(a, b):
    return lax.dot_general(a, b, (((1,), (1,)), ((), ())), preferred_element_type=F32)


def count_hits(hits, count, z, y, core):
    lane = lax.broadcasted_iota(jnp.int32, (HITS, TILE), 1)
    block_of_lane = lax.rem(lane, BLOCKS).astype(F32)
    quarter = lane // BLOCKS
    tile_of_row = lax.broadcasted_iota(jnp.int32, (BANK, 2 * TILE), 0).astype(F32)
    for kind in range(2):
        first, step = (z * 8 + core, 2) if kind == 0 else (y * 2 + core, 8)
        source = lax.broadcasted_iota(jnp.int32, (GROUP, COLS * TILE), 0)
        column = lax.broadcasted_iota(jnp.int32, (GROUP, COLS * TILE), 1) // TILE
        choose = jnp.where(source == first + step * column, 1.0, 0.0).astype(BF16)
        for m in range(MATS):
            spread = []
            for which in range(3):
                if kind == 0:
                    rows = [
                        hits[which, m, pl.ds(zz * 8 + y * 2, 2)].reshape(2 * HITS, GROUP)
                        for zz in range(4)
                    ]
                    values = jnp.concatenate(rows, axis=0)
                else:
                    values = hits[which, m, pl.ds(z * 8, ROWS)].reshape(ROWS * HITS, GROUP)
                spread.append(dot(values.astype(F32).astype(BF16), choose))

            def lanes_of(values, col, half):
                parts = [
                    values[(half * 4 + q) * HITS : (half * 4 + q + 1) * HITS, col * TILE : (col + 1) * TILE]
                    for q in range(4)
                ]
                low = jnp.where(quarter == 0, parts[0], parts[1])
                high = jnp.where(quarter == 2, parts[2], parts[3])
                return jnp.where(quarter < 2, low, high)

            for col in range(COLS):
                tile_rows, sign_rows = [], []
                for half in range(2):
                    tile, block, sign = [lanes_of(values, col, half) for values in spread]
                    tile_rows.append(jnp.where(block == block_of_lane, tile, -1.0))
                    sign_rows.append(2.0 * sign - 1.0)
                tile_rows = jnp.concatenate(tile_rows, axis=1)
                sign_rows = jnp.concatenate(sign_rows, axis=1)
                total = jnp.zeros((BANK, 2 * TILE), F32)
                for h in range(HITS):
                    total += jnp.where(
                        tile_of_row == tile_rows[h : h + 1, :], sign_rows[h : h + 1, :], 0.0
                    )
                at = (m * COLS + col) * BANK
                count[kind, at : at + BANK, :] = total.astype(BF16)


def turn_bank(bank, bank_t):
    def turn(r, carry):
        bank_t[pl.ds(r, TILE, stride=BANK), :] = bank[r].astype(F32).T
        return carry

    lax.fori_loop(0, BANK, turn, 0, unroll=4)


def turn_rows(ins, left32, left, e):
    def turn(i, carry):
        left32[pl.ds(i, TILE, stride=ROWS), :] = ins[e, i].astype(F32).T
        return carry

    lax.fori_loop(0, ROWS, turn, 0, unroll=4)
    left[...] = left32[...].astype(BF16)


def gradient(left, cots, grads, e, slot):
    rows = left[...]
    for m in range(MATS):
        halves = []
        for col in range(0, COLS, 2):
            right = jnp.concatenate([cots[e, col, m], cots[e, col + 1, m]], axis=1)
            halves.append(dot(rows, right).reshape(TILE, ROWS, 2 * TILE))
        at = (slot * MATS + m) * 2 * ROWS
        grads[:, at : at + 2 * ROWS, :] = jnp.concatenate(halves, axis=1).astype(BF16)


def project(grads, bank_t, quads):
    def step(two, carry):
        outs = []
        for u in range(2):
            a = two * 2 + u
            tiles = bank_t[pl.ds(pl.multiple_of(a * BANK, BANK), BANK), :].astype(BF16)
            zero = jnp.zeros_like(tiles)
            weights = jnp.concatenate(
                [jnp.concatenate([tiles, zero], axis=1), jnp.concatenate([zero, tiles], axis=1)], axis=0
            )
            outs.append(dot_nt(grads[a], weights))
        at = pl.multiple_of(two * 2 * ROWS, 2 * ROWS)
        for slot in range(EX):
            for pair in range(PAIRS):
                src = (slot * PAIRS + pair) * ROWS
                both = jnp.concatenate([out[src : src + ROWS] for out in outs], axis=0)
                quads[slot, pl.ds(at, 2 * ROWS), pair * TILE : (pair + 1) * TILE] = both.astype(BF16)
        return carry

    lax.fori_loop(0, TILE // 2, step, 0, unroll=16)


def select(quads, count, picked, slot, kind):
    row_in_group = lax.rem(lax.broadcasted_iota(jnp.int32, (TILE * ROWS, TILE), 0), ROWS)
    lane_group = lax.broadcasted_iota(jnp.int32, (TILE * ROWS, TILE), 1) // BLOCKS
    sums = dot(quads[slot], count[kind])
    folded = jnp.where(row_in_group >= 4, sums[:, TILE:], sums[:, :TILE])
    picked[...] = jnp.where(lane_group == lax.rem(row_in_group, 4), folded, 0.0)
    total = picked[pl.ds(0, TILE, stride=ROWS), :]
    for i in range(1, ROWS):
        total += picked[pl.ds(i, TILE, stride=ROWS), :]
    turned = total.T
    return turned[0:32] + turned[32:64] + turned[64:96] + turned[96:128]


class Ring:
    def __init__(self, source, slots, slot_of, send, recv, pos, to):
        self.slots, self.slot_of, self.send, self.recv = slots, slot_of, send, recv
        self.pos, self.to, self.source = pos, to, source
        self.copies = []

    def _copy(self, src, dst, index, direction):
        copy = pltpu.make_async_remote_copy(
            src_ref=src,
            dst_ref=dst,
            send_sem=self.send.at[index],
            recv_sem=self.recv.at[index],
            device_id={"param": self.to(direction)},
            device_id_type=MESH,
        )
        copy.start()
        self.copies.append(copy)

    def slot(self, offset):
        return self.slot_of(lax.rem(self.pos + offset + 4, 4))

    def start(self):
        mine = self.slots.at[self.slot(0)]
        self._copy(self.source, mine, 0, 1)
        self._copy(self.source, mine, 1, -1)

    def hand_on(self):
        half = TOK // 2
        for way in range(2):
            self.copies[way].wait_recv()
            came_from = self.slots.at[self.slot(-1 if way == 0 else 1)]
            tokens = pl.ds(way * half, half)
            piece = came_from.at[:, tokens] if len(came_from.shape) == 3 else came_from.at[tokens]
            self._copy(piece, piece, 2 + way, 1 if way == 0 else -1)

    def finish(self):
        self.copies[2].wait_recv()
        self.copies[3].wait_recv()


def kernel(
    in_hbm, cot_hbm, bank_hbm, tiles_hbm, blocks_hbm, signs_hbm, test_hbm, out_ref,
    bank, bank_t, hits, cots, ins, left32, left, grads, quads, picked, count, tests,
    raw, raw_in, part, part_in, done,
    load_sem, own_sem, j_send, j_recv, i_send, i_recv, p_send, p_recv, t_send, t_recv, ex_send, ex_recv,
):
    me = lax.axis_index("param")
    mx = lax.axis_index("ex")
    core = lax.rem(me, 2)
    y = lax.rem(me // 2, 4)
    z = me // 8

    def device(zz, yy, cc):
        return (zz * 4 + yy) * 2 + cc

    loads = [
        pltpu.make_async_copy(tiles_hbm, hits.at[0], load_sem.at[0]),
        pltpu.make_async_copy(blocks_hbm, hits.at[1], load_sem.at[1]),
        pltpu.make_async_copy(signs_hbm, hits.at[2], load_sem.at[2]),
        pltpu.make_async_copy(bank_hbm, bank, load_sem.at[3]),
        pltpu.make_async_copy(test_hbm, tests.at[mx], load_sem.at[4]),
    ]
    for copy in loads:
        copy.start()
    row_slot = [z * 2 + core, z * 2 + core, y * 2 + core, y * 2 + core]
    col_slot = [y, y, z, z]
    own = []
    for e in range(EX):
        own.append(pltpu.make_async_copy(in_hbm.at[e], ins.at[e, row_slot[e]], own_sem.at[e, 0]))
        own.append(pltpu.make_async_copy(cot_hbm.at[:, e], cots.at[e, col_slot[e]], own_sem.at[e, 1]))
    for copy in own:
        copy.start()

    barrier = pltpu.get_barrier_semaphore()

    def greet(d, carry):
        pl.semaphore_signal(
            barrier, inc=1, device_id={"param": lax.rem(me + d, GROUP)}, device_id_type=MESH
        )
        return carry

    lax.fori_loop(1, GROUP, greet, 0)
    for d in range(1, 4):
        pl.semaphore_signal(barrier, inc=1, device_id={"ex": lax.rem(mx + d, 4)}, device_id_type=MESH)
    pl.semaphore_wait(barrier, GROUP - 1 + 3)

    cols, rows, relays = {}, {}, {}
    sibling = device(z, y, 1 - core)

    def along_y(direction):
        return device(z, lax.rem(y + direction + 4, 4), core)

    def along_z(direction):
        return device(lax.rem(z + direction + 4, 4), y, core)

    def relay(e, index, offset):
        slot = rows[e].slot(offset)
        copy = pltpu.make_async_remote_copy(
            src_ref=ins.at[e, slot],
            dst_ref=ins.at[e, slot],
            send_sem=p_send.at[e, index],
            recv_sem=p_recv.at[e, index],
            device_id={"param": sibling},
            device_id_type=MESH,
        )
        copy.start()
        relays[e, index] = copy

    for e in ORDER:
        col_pos, col_to, row_pos, row_to = (y, along_y, z, along_z) if e < 2 else (z, along_z, y, along_y)
        cols[e] = Ring(
            cot_hbm.at[:, e], cots.at[e], lambda pos: pos, j_send.at[e], j_recv.at[e], col_pos, col_to
        )
        rows[e] = Ring(
            in_hbm.at[e], ins.at[e], lambda pos: pos * 2 + core, i_send.at[e], i_recv.at[e], row_pos, row_to
        )
        rows[e].start()
        cols[e].start()
    test_copies = []
    for d in range(1, 4):
        copy = pltpu.make_async_remote_copy(
            src_ref=test_hbm,
            dst_ref=tests.at[mx],
            send_sem=t_send.at[d - 1],
            recv_sem=t_recv.at[d - 1],
            device_id={"ex": lax.rem(mx + d, 4)},
            device_id_type=MESH,
        )
        copy.start()
        test_copies.append(copy)

    for copy in own:
        copy.wait()
    for e in ORDER:
        relay(e, 0, 0)
    for copy in loads:
        copy.wait()

    def hand_on(e):
        rows[e].hand_on()
        relay(e, 1, -1)
        relay(e, 2, 1)
        cols[e].hand_on()

    count_hits(hits, count, z, y, core)
    hand_on(ORDER[0])
    hand_on(ORDER[1])
    turn_bank(bank, bank_t)
    hand_on(ORDER[2])
    hand_on(ORDER[3])
    raw[...] = jnp.zeros_like(raw)
    for e in ORDER:
        rows[e].finish()
        relay(e, 3, 2)
    for slot, e in enumerate(ORDER):
        for index in range(4):
            relays[e, index].wait_recv()
        turn_rows(ins, left32, left, e)
        cols[e].finish()
        gradient(left, cots, grads, e, slot)
    project(grads, bank_t, quads)
    for slot, e in enumerate(ORDER):
        raw[pl.ds(e, BLOCKS, stride=8), :] = select(quads, count, picked, slot, 0 if e < 2 else 1)

    def exchange(index, source, target):
        def copy(d):
            return pltpu.make_async_remote_copy(
                src_ref=source(lax.rem(me + d, GROUP)),
                dst_ref=target,
                send_sem=ex_send.at[index, d],
                recv_sem=ex_recv.at[index, d],
                device_id={"param": lax.rem(me + d, GROUP)},
                device_id_type=MESH,
            )

        def start(d, carry):
            copy(d).start()
            return carry

        def wait(d, carry):
            copy(d).wait_recv()
            return carry

        def drain(d, carry):
            copy(d).wait_send()
            return carry

        lax.fori_loop(1, GROUP, start, 0)
        lax.fori_loop(1, GROUP, wait, 0)
        return lambda: lax.fori_loop(1, GROUP, drain, 0)

    raw_in[me] = raw[pl.ds(pl.multiple_of(me * 8, 8), 8), :]
    drains = [
        exchange(0, lambda to: raw.at[pl.ds(pl.multiple_of(to * 8, 8), 8), :], raw_in.at[me])
    ]
    features = jnp.sum(raw_in[...], axis=0) * SCALE
    high = features.astype(BF16)
    low = (features - high.astype(F32)).astype(BF16)
    both = jnp.concatenate([high, low], axis=0)
    for copy in test_copies:
        copy.wait_recv()
    for quarter_of in range(4):
        scores = dot_nt(both, tests[quarter_of])
        scores = scores[:8] + scores[8:]
        for half in range(2):
            for e in range(EX):
                part[(quarter_of * 2 + half) * EX + e] = scores[e : e + 1, half * TILE : (half + 1) * TILE]
    part_in[me] = part[me]
    drains.append(exchange(1, lambda to: part.at[to], part_in.at[me]))
    done[me] = jnp.sum(part_in[...], axis=0)
    drains.append(exchange(2, lambda to: done.at[me], done.at[me]))
    for chunk in range(8):
        for e in range(EX):
            out_ref[e : e + 1, chunk * TILE : (chunk + 1) * TILE] = done[chunk * EX + e]
    for drain in drains:
        drain()
    for ring in list(cols.values()) + list(rows.values()):
        for copy in ring.copies:
            copy.wait_send()
    for copy in list(relays.values()) + test_copies:
        copy.wait_send()


def local(inputs, cotangents, jl_bank, jl_tiles, jl_blocks, jl_signs, test_features):
    turned = [jnp.transpose(a, (0, 1, 3, 2)) for a in (jl_tiles, jl_blocks, jl_signs)]
    anywhere = pl.BlockSpec(memory_space=pl.ANY)
    dma = pltpu.SemaphoreType.DMA
    return pl.pallas_call(
        kernel,
        out_shape=jax.ShapeDtypeStruct((EX, 1024), F32),
        in_specs=[anywhere] * 7,
        out_specs=pl.BlockSpec(memory_space=pltpu.VMEM),
        scratch_shapes=[
            pltpu.VMEM((BANK, TILE, TILE), BF16),
            pltpu.VMEM((TILE * BANK, TILE), F32),
            pltpu.VMEM((3, MATS, GROUP, HITS, GROUP), jnp.int32),
            pltpu.VMEM((EX, COLS, MATS, TOK, TILE), BF16),
            pltpu.VMEM((EX, ROWS, TOK, TILE), BF16),
            pltpu.VMEM((TILE * ROWS, TOK), F32),
            pltpu.VMEM((TILE * ROWS, TOK), BF16),
            pltpu.VMEM((TILE, EX * PAIRS * ROWS, 2 * TILE), BF16),
            pltpu.VMEM((EX, TILE * ROWS, PAIRS * TILE), BF16),
            pltpu.VMEM((TILE * ROWS, TILE), F32),
            pltpu.VMEM((2, MATS * COLS * BANK, 2 * TILE), BF16),
            pltpu.VMEM((4, 256, TILE), BF16),
            pltpu.VMEM((BLOCKS * 8, TILE), F32),
            pltpu.VMEM((GROUP, 8, TILE), F32),
            pltpu.VMEM((GROUP, 1, TILE), F32),
            pltpu.VMEM((GROUP, 1, TILE), F32),
            pltpu.VMEM((GROUP, 1, TILE), F32),
            dma((5,)),
            dma((EX, 2)),
            dma((EX, 4)),
            dma((EX, 4)),
            dma((EX, 4)),
            dma((EX, 4)),
            dma((EX, 4)),
            dma((EX, 4)),
            dma((3,)),
            dma((3,)),
            dma((3, GROUP)),
            dma((3, GROUP)),
        ],
        compiler_params=pltpu.CompilerParams(
            collective_id=0, has_side_effects=True, vmem_limit_bytes=56 * 1024 * 1024
        ),
        cost_estimate=pl.CostEstimate(flops=9_000_000_000, bytes_accessed=8_000_000, transcendentals=0),
    )(inputs, cotangents, jl_bank, *turned, test_features)


def solution(mesh):
    placed = (
        P("ex", None, "param"),
        P(None, "ex", None, "param"),
        P(),
        P(),
        P(),
        P(),
        P("ex", "param"),
    )
    return jax.shard_map(
        local, mesh=mesh, in_specs=placed, out_specs=P("ex", None), check_vma=False
    )
```

time: 63.5 us -> 52.4 us (0.83)
  Pallas kernels: 62 us -> 50.9 us
    pallas_call x1, Pallas kernels: 62 us -> 50.9 us  [local(): pl.pallas_call(kernel, out_shape=jax.ShapeDtypeStruct((EX, 1024), F32), i...]
where the time goes in v2:
time: 52.4 us; the launch traced here: 52.3 us
  Pallas kernels  50.9 us (97%)
  local copies, waits for them, and re-layouts  1.32 us (3%)
    pallas_call x1, Pallas kernels, local(): pl.pallas_call(kernel, out_shape=jax.ShapeDtypeStruct((EX, 1024), F32), i...  50.9 us
    unnamed x1, local copies, waits for them, and re-layouts  1.32 us

profile of v2, /device:TPU:1, one launch (start us, length us, event | category | flops | bytes accessed | tf_op | source)
XLA Modules:
  0.0 52.3 jit_solution(6179847568137010149)
XLA Ops:
  0.0 50.9 %shard_map.73 = f32[4,1024]{1,0:T(4,128)} custom-call(bf16[4,128,128]{2,1,0:T(8,128)(2,1)} %in_hbm.1, bf16[3,4,128,128]{3,2,1,0:T(8,128)(2,1)} %cot_hbm.1, bf16[64,128,128]{2,1,0:T(8,128)(2,1)} %bank_hbm.1, s32[3,32,8,32]{3,2,1,0:T(8,128)} %bitcast.3, s32[3,32,8,32]{3,2,1,0:T(8,128)} %bitcast.4, s32[3,32,8,32]{3,2,1,0:T(8,128)} %bitcast.5, ...), custom_call_target="tpu_custom_call" | custom-call | flops 8999999488 | bytes 8000000 | tf_op jit(solution)/shard_map/pallas_call | solution.py:378
  50.9 1.3 %copy.9 = f32[4,1024]{1,0:T(4,128)} copy(f32[4,1024]{1,0:T(4,128)} %shard_map.73) | data formatting | bytes 32768

commit v3 on v2

--- a/solution.py
+++ b/solution.py
@@ -149,9 +149,9 @@
 
 
 class Ring:
-    def __init__(self, source, slots, slot_of, send, recv, pos, to):
-        self.slots, self.slot_of, self.send, self.recv = slots, slot_of, send, recv
-        self.pos, self.to, self.source = pos, to, source
+    def __init__(self, source, place, send, recv, pos, to):
+        self.source, self.place, self.send, self.recv = source, place, send, recv
+        self.pos, self.to = pos, to
         self.copies = []
 
     def _copy(self, src, dst, index, direction):
@@ -166,21 +166,18 @@
         copy.start()
         self.copies.append(copy)
 
-    def slot(self, offset):
-        return self.slot_of(lax.rem(self.pos + offset + 4, 4))
+    def at(self, offset):
+        return self.place(lax.rem(self.pos + offset + 4, 4))
 
     def start(self):
-        mine = self.slots.at[self.slot(0)]
-        self._copy(self.source, mine, 0, 1)
-        self._copy(self.source, mine, 1, -1)
+        self._copy(self.source, self.at(0), 0, 1)
+        self._copy(self.source, self.at(0), 1, -1)
 
     def hand_on(self):
         half = TOK // 2
         for way in range(2):
             self.copies[way].wait_recv()
-            came_from = self.slots.at[self.slot(-1 if way == 0 else 1)]
-            tokens = pl.ds(way * half, half)
-            piece = came_from.at[:, tokens] if len(came_from.shape) == 3 else came_from.at[tokens]
+            piece = self.at(-1 if way == 0 else 1).at[:, pl.ds(way * half, half)]
             self._copy(piece, piece, 2 + way, 1 if way == 0 else -1)
 
     def finish(self):
@@ -192,7 +189,7 @@
     in_hbm, cot_hbm, bank_hbm, tiles_hbm, blocks_hbm, signs_hbm, test_hbm, out_ref,
     bank, bank_t, hits, cots, ins, left32, left, grads, quads, picked, count, tests,
     raw, raw_in, part, part_in, done,
-    load_sem, own_sem, j_send, j_recv, i_send, i_recv, p_send, p_recv, t_send, t_recv, ex_send, ex_recv,
+    load_sem, own_sem, j_send, j_recv, i_send, i_recv, p_send, p_recv, t_send, t_recv, ex_send, ex_recv, ready,
 ):
     me = lax.axis_index("param")
     mx = lax.axis_index("ex")
@@ -203,70 +200,83 @@
     def device(zz, yy, cc):
         return (zz * 4 + yy) * 2 + cc
 
+    def along_y(direction):
+        return device(z, lax.rem(y + direction + 4, 4), core)
+
+    def along_z(direction):
+        return device(lax.rem(z + direction + 4, 4), y, core)
+
+    sibling = device(z, y, 1 - core)
+
+    barrier = pltpu.get_barrier_semaphore()
+    for to in (along_y(1), along_y(-1), along_z(1), along_z(-1), sibling):
+        pl.semaphore_signal(barrier, inc=1, device_id={"param": to}, device_id_type=MESH)
+    for d in range(1, 4):
+        pl.semaphore_signal(barrier, inc=1, device_id={"ex": lax.rem(mx + d, 4)}, device_id_type=MESH)
+
     loads = [
         pltpu.make_async_copy(tiles_hbm, hits.at[0], load_sem.at[0]),
         pltpu.make_async_copy(blocks_hbm, hits.at[1], load_sem.at[1]),
         pltpu.make_async_copy(signs_hbm, hits.at[2], load_sem.at[2]),
         pltpu.make_async_copy(bank_hbm, bank, load_sem.at[3]),
-        pltpu.make_async_copy(test_hbm, tests.at[mx], load_sem.at[4]),
     ]
     for copy in loads:
         copy.start()
-    row_slot = [z * 2 + core, z * 2 + core, y * 2 + core, y * 2 + core]
-    col_slot = [y, y, z, z]
-    own = []
-    for e in range(EX):
-        own.append(pltpu.make_async_copy(in_hbm.at[e], ins.at[e, row_slot[e]], own_sem.at[e, 0]))
-        own.append(pltpu.make_async_copy(cot_hbm.at[:, e], cots.at[e, col_slot[e]], own_sem.at[e, 1]))
+    own = [pltpu.make_async_copy(test_hbm, tests.at[mx], load_sem.at[4])]
+    for kind in range(2):
+        pair = pl.ds(2 * kind, 2)
+        col_pos, row_pos = (y, z) if kind == 0 else (z, y)
+        own.append(
+            pltpu.make_async_copy(
+                in_hbm.at[pair], ins.at[pair, row_pos * 2 + core], own_sem.at[kind]
+            )
+        )
+        for e in (2 * kind, 2 * kind + 1):
+            own.append(
+                pltpu.make_async_copy(cot_hbm.at[:, e], cots.at[e, col_pos], own_sem.at[2 + e])
+            )
     for copy in own:
         copy.start()
 
-    barrier = pltpu.get_barrier_semaphore()
-
-    def greet(d, carry):
-        pl.semaphore_signal(
-            barrier, inc=1, device_id={"param": lax.rem(me + d, GROUP)}, device_id_type=MESH
-        )
-        return carry
-
-    lax.fori_loop(1, GROUP, greet, 0)
-    for d in range(1, 4):
-        pl.semaphore_signal(barrier, inc=1, device_id={"ex": lax.rem(mx + d, 4)}, device_id_type=MESH)
-    pl.semaphore_wait(barrier, GROUP - 1 + 3)
-
-    cols, rows, relays = {}, {}, {}
-    sibling = device(z, y, 1 - core)
-
-    def along_y(direction):
-        return device(z, lax.rem(y + direction + 4, 4), core)
-
-    def along_z(direction):
-        return device(lax.rem(z + direction + 4, 4), y, core)
-
-    def relay(e, index, offset):
-        slot = rows[e].slot(offset)
+    for copy in loads[:3]:
+        copy.wait()
+    count_hits(hits, count, z, y, core)
+    loads[3].wait()
+    turn_bank(bank, bank_t)
+    raw[...] = jnp.zeros_like(raw)
+    pl.semaphore_wait(barrier, 5 + 3)
+
+    cols, rows, relays, tests_out = {}, {}, {}, []
+
+    def relay(kind, index, offset):
+        place = rows[kind].at(offset)
         copy = pltpu.make_async_remote_copy(
-            src_ref=ins.at[e, slot],
-            dst_ref=ins.at[e, slot],
-            send_sem=p_send.at[e, index],
-            recv_sem=p_recv.at[e, index],
+            src_ref=rows[kind].source if index == 0 else place,
+            dst_ref=place,
+            send_sem=p_send.at[kind, index],
+            recv_sem=p_recv.at[kind, index],
             device_id={"param": sibling},
             device_id_type=MESH,
         )
         copy.start()
-        relays[e, index] = copy
-
+        relays[kind, index] = copy
+
+    for kind in range(2):
+        pair = pl.ds(2 * kind, 2)
+        pos, to = (z, along_z) if kind == 0 else (y, along_y)
+        rows[kind] = Ring(
+            in_hbm.at[pair], lambda at, pair=pair: ins.at[pair, at * 2 + core],
+            i_send.at[kind], i_recv.at[kind], pos, to,
+        )
+        rows[kind].start()
     for e in ORDER:
-        col_pos, col_to, row_pos, row_to = (y, along_y, z, along_z) if e < 2 else (z, along_z, y, along_y)
+        pos, to = (y, along_y) if e < 2 else (z, along_z)
         cols[e] = Ring(
-            cot_hbm.at[:, e], cots.at[e], lambda pos: pos, j_send.at[e], j_recv.at[e], col_pos, col_to
-        )
-        rows[e] = Ring(
-            in_hbm.at[e], ins.at[e], lambda pos: pos * 2 + core, i_send.at[e], i_recv.at[e], row_pos, row_to
-        )
-        rows[e].start()
+            cot_hbm.at[:, e], lambda at, e=e: cots.at[e, at], j_send.at[e], j_recv.at[e], pos, to
+        )
         cols[e].start()
-    test_copies = []
+    for kind in range(2):
+        relay(kind, 0, 0)
     for d in range(1, 4):
         copy = pltpu.make_async_remote_copy(
             src_ref=test_hbm,
@@ -277,77 +287,60 @@
             device_id_type=MESH,
         )
         copy.start()
-        test_copies.append(copy)
-
+        tests_out.append(copy)
     for copy in own:
         copy.wait()
-    for e in ORDER:
-        relay(e, 0, 0)
-    for copy in loads:
-        copy.wait()
-
-    def hand_on(e):
-        rows[e].hand_on()
-        relay(e, 1, -1)
-        relay(e, 2, 1)
-        cols[e].hand_on()
-
-    count_hits(hits, count, z, y, core)
-    hand_on(ORDER[0])
-    hand_on(ORDER[1])
-    turn_bank(bank, bank_t)
-    hand_on(ORDER[2])
-    hand_on(ORDER[3])
-    raw[...] = jnp.zeros_like(raw)
-    for e in ORDER:
-        rows[e].finish()
-        relay(e, 3, 2)
+
+    for kind in range(2):
+        rows[kind].hand_on()
+        relay(kind, 1, -1)
+        relay(kind, 2, 1)
+    cols[ORDER[0]].hand_on()
+    cols[ORDER[1]].hand_on()
+    for kind in range(2):
+        rows[kind].finish()
+        relay(kind, 3, 2)
+    cols[ORDER[2]].hand_on()
     for slot, e in enumerate(ORDER):
-        for index in range(4):
-            relays[e, index].wait_recv()
+        if slot == 1:
+            cols[ORDER[3]].hand_on()
+        kind = e // 2
+        if e % 2 == 0:
+            for index in range(4):
+                relays[kind, index].wait_recv()
         turn_rows(ins, left32, left, e)
         cols[e].finish()
         gradient(left, cots, grads, e, slot)
+    pl.semaphore_signal(ready, inc=1, device_id={"param": sibling}, device_id_type=MESH)
     project(grads, bank_t, quads)
     for slot, e in enumerate(ORDER):
-        raw[pl.ds(e, BLOCKS, stride=8), :] = select(quads, count, picked, slot, 0 if e < 2 else 1)
-
-    def exchange(index, source, target):
-        def copy(d):
-            return pltpu.make_async_remote_copy(
-                src_ref=source(lax.rem(me + d, GROUP)),
-                dst_ref=target,
-                send_sem=ex_send.at[index, d],
-                recv_sem=ex_recv.at[index, d],
-                device_id={"param": lax.rem(me + d, GROUP)},
+        raw[pl.ds(e, BLOCKS, stride=8), :] = select(quads, count, picked, slot, e // 2)
+
+    def exchange(index, source, incoming):
+        for d in range(1, GROUP):
+            to = lax.rem(me + d, GROUP)
+            pltpu.make_async_remote_copy(
+                src_ref=source(to),
+                dst_ref=incoming.at[me],
+                send_sem=ex_send.at[index],
+                recv_sem=ex_recv.at[index],
+                device_id={"param": to},
                 device_id_type=MESH,
-            )
-
-        def start(d, carry):
-            copy(d).start()
-            return carry
-
-        def wait(d, carry):
-            copy(d).wait_recv()
-            return carry
-
-        def drain(d, carry):
-            copy(d).wait_send()
-            return carry
-
-        lax.fori_loop(1, GROUP, start, 0)
-        lax.fori_loop(1, GROUP, wait, 0)
-        return lambda: lax.fori_loop(1, GROUP, drain, 0)
-
+            ).start()
+        others = incoming.at[pl.ds(0, GROUP - 1)]
+        pltpu.make_async_copy(others, others, ex_recv.at[index]).wait()
+        return lambda: pltpu.make_async_copy(others, others, ex_send.at[index]).wait()
+
+    pl.semaphore_wait(ready, 1)
     raw_in[me] = raw[pl.ds(pl.multiple_of(me * 8, 8), 8), :]
     drains = [
-        exchange(0, lambda to: raw.at[pl.ds(pl.multiple_of(to * 8, 8), 8), :], raw_in.at[me])
+        exchange(0, lambda to: raw.at[pl.ds(pl.multiple_of(to * 8, 8), 8), :], raw_in)
     ]
     features = jnp.sum(raw_in[...], axis=0) * SCALE
     high = features.astype(BF16)
     low = (features - high.astype(F32)).astype(BF16)
     both = jnp.concatenate([high, low], axis=0)
-    for copy in test_copies:
+    for copy in tests_out:
         copy.wait_recv()
     for quarter_of in range(4):
         scores = dot_nt(both, tests[quarter_of])
@@ -356,9 +349,9 @@
             for e in range(EX):
                 part[(quarter_of * 2 + half) * EX + e] = scores[e : e + 1, half * TILE : (half + 1) * TILE]
     part_in[me] = part[me]
-    drains.append(exchange(1, lambda to: part.at[to], part_in.at[me]))
+    drains.append(exchange(1, lambda to: part.at[to], part_in))
     done[me] = jnp.sum(part_in[...], axis=0)
-    drains.append(exchange(2, lambda to: done.at[me], done.at[me]))
+    drains.append(exchange(2, lambda to: done.at[me], done))
     for chunk in range(8):
         for e in range(EX):
             out_ref[e : e + 1, chunk * TILE : (chunk + 1) * TILE] = done[chunk * EX + e]
@@ -367,7 +360,7 @@
     for ring in list(cols.values()) + list(rows.values()):
         for copy in ring.copies:
             copy.wait_send()
-    for copy in list(relays.values()) + test_copies:
+    for copy in list(relays.values()) + tests_out:
         copy.wait_send()
 
 
@@ -399,17 +392,18 @@
             pltpu.VMEM((GROUP, 1, TILE), F32),
             pltpu.VMEM((GROUP, 1, TILE), F32),
             dma((5,)),
-            dma((EX, 2)),
+            dma((2 + EX,)),
             dma((EX, 4)),
             dma((EX, 4)),
-            dma((EX, 4)),
-            dma((EX, 4)),
-            dma((EX, 4)),
-            dma((EX, 4)),
+            dma((2, 4)),
+            dma((2, 4)),
+            dma((2, 4)),
+            dma((2, 4)),
             dma((3,)),
             dma((3,)),
-            dma((3, GROUP)),
-            dma((3, GROUP)),
+            dma((3,)),
+            dma((3,)),
+            pltpu.SemaphoreType.REGULAR,
         ],
         compiler_params=pltpu.CompilerParams(
             collective_id=0, has_side_effects=True, vmem_limit_bytes=56 * 1024 * 1024

time: 52.4 us -> 49.9 us (0.952)
  Pallas kernels: 50.9 us -> 48.4 us
    pallas_call x1, Pallas kernels: 50.9 us -> 48.4 us  [local(): pl.pallas_call(kernel, out_shape=jax.ShapeDtypeStruct((EX, 1024), F32), i...]
where the time goes in v3:
time: 49.9 us; the launch traced here: 49.7 us
  Pallas kernels  48.4 us (97%)
  local copies, waits for them, and re-layouts  1.32 us (3%)
    pallas_call x1, Pallas kernels, local(): pl.pallas_call(kernel, out_shape=jax.ShapeDtypeStruct((EX, 1024), F32), i...  48.4 us
    unnamed x1, local copies, waits for them, and re-layouts  1.32 us

profile of v3, /device:TPU:1, one launch (start us, length us, event | category | flops | bytes accessed | tf_op | source)
XLA Modules:
  0.0 49.7 jit_solution(11963814432688321682)
XLA Ops:
  0.0 48.4 %shard_map.73 = f32[4,1024]{1,0:T(4,128)} custom-call(bf16[4,128,128]{2,1,0:T(8,128)(2,1)} %in_hbm.1, bf16[3,4,128,128]{3,2,1,0:T(8,128)(2,1)} %cot_hbm.1, bf16[64,128,128]{2,1,0:T(8,128)(2,1)} %bank_hbm.1, s32[3,32,8,32]{3,2,1,0:T(8,128)} %bitcast.3, s32[3,32,8,32]{3,2,1,0:T(8,128)} %bitcast.4, s32[3,32,8,32]{3,2,1,0:T(8,128)} %bitcast.5, ...), custom_call_target="tpu_custom_call" | custom-call | flops 8999999488 | bytes 8000000 | tf_op jit(solution)/shard_map/pallas_call | solution.py:371
  48.4 1.3 %copy.9 = f32[4,1024]{1,0:T(4,128)} copy(f32[4,1024]{1,0:T(4,128)} %shard_map.73) | data formatting | bytes 32768

commit v4 on v3

v4 whole, which is shorter than its diff:
```python
import functools
import math

import jax
import jax.numpy as jnp
from jax import lax
from jax.experimental import pallas as pl
from jax.experimental.pallas import tpu as pltpu
from jax.sharding import PartitionSpec as P

D = 4096
K = 4096
TILE = 128
HITS = 8
MATS = 3
TOK = 128
BANK = 64
BLOCKS = 32
EX = 4
ROWS = 8
COLS = 4
PAIRS = MATS * COLS // 2
GROUP = 32
BATCH = 2
MESH = pl.DeviceIdType.MESH
F32 = jnp.float32
BF16 = jnp.bfloat16
SCALE = 1.0 / (math.sqrt(TOK * MATS * HITS * D * D / (TILE * K)) * math.sqrt(K))
ORDER = (0, 2, 1, 3)


def dot(a, b):
    return lax.dot_general(a, b, (((1,), (0,)), ((), ())), preferred_element_type=F32)


def dot_nt(a, b):
    return lax.dot_general(a, b, (((1,), (1,)), ((), ())), preferred_element_type=F32)


def count_hits(hits, count, z, y, core):
    lane = lax.broadcasted_iota(jnp.int32, (HITS, TILE), 1)
    block_of_lane = lax.rem(lane, BLOCKS).astype(F32)
    quarter = lane // BLOCKS
    tile_of_row = lax.broadcasted_iota(jnp.int32, (BANK, 2 * TILE), 0).astype(F32)
    for kind in range(2):
        first, step = (z * 8 + core, 2) if kind == 0 else (y * 2 + core, 8)
        source = lax.broadcasted_iota(jnp.int32, (GROUP, COLS * TILE), 0)
        column = lax.broadcasted_iota(jnp.int32, (GROUP, COLS * TILE), 1) // TILE
        choose = jnp.where(source == first + step * column, 1.0, 0.0).astype(BF16)
        for m in range(MATS):
            spread = []
            for which in range(3):
                if kind == 0:
                    rows = [
                        hits[which, m, pl.ds(zz * 8 + y * 2, 2)].reshape(2 * HITS, GROUP)
                        for zz in range(4)
                    ]
                    values = jnp.concatenate(rows, axis=0)
                else:
                    values = hits[which, m, pl.ds(z * 8, ROWS)].reshape(ROWS * HITS, GROUP)
                spread.append(dot(values.astype(F32).astype(BF16), choose))

            def lanes_of(values, col, half):
                parts = [
                    values[(half * 4 + q) * HITS : (half * 4 + q + 1) * HITS, col * TILE : (col + 1) * TILE]
                    for q in range(4)
                ]
                low = jnp.where(quarter == 0, parts[0], parts[1])
                high = jnp.where(quarter == 2, parts[2], parts[3])
                return jnp.where(quarter < 2, low, high)

            for col in range(COLS):
                tile_rows, sign_rows = [], []
                for half in range(2):
                    tile, block, sign = [lanes_of(values, col, half) for values in spread]
                    tile_rows.append(jnp.where(block == block_of_lane, tile, -1.0))
                    sign_rows.append(2.0 * sign - 1.0)
                tile_rows = jnp.concatenate(tile_rows, axis=1)
                sign_rows = jnp.concatenate(sign_rows, axis=1)
                total = jnp.zeros((BANK, 2 * TILE), F32)
                for h in range(HITS):
                    total += jnp.where(
                        tile_of_row == tile_rows[h : h + 1, :], sign_rows[h : h + 1, :], 0.0
                    )
                at = (m * COLS + col) * BANK
                count[kind, at : at + BANK, :] = total.astype(BF16)


def turn_bank(bank, bank_t):
    def turn(r, carry):
        bank_t[pl.ds(r, TILE, stride=BANK), :] = bank[r].astype(F32).T
        return carry

    lax.fori_loop(0, BANK, turn, 0, unroll=4)


def turn_rows(ins, left32, left, e):
    def turn(i, carry):
        left32[pl.ds(i, TILE, stride=ROWS), :] = ins[e, i].astype(F32).T
        return carry

    lax.fori_loop(0, ROWS, turn, 0, unroll=4)
    left[...] = left32[...].astype(BF16)


def spread_bank(bank_t, weights):
    lower = lax.broadcasted_iota(jnp.int32, (TILE, 2 * BANK), 1) < BANK

    def step(a, carry):
        tiles = bank_t[pl.ds(pl.multiple_of(a * BANK, BANK), BANK), :]
        turned = jnp.concatenate([tiles, tiles], axis=0).T
        weights[a, 0:TILE] = jnp.where(lower, turned, 0.0).astype(BF16)
        weights[a, TILE:] = jnp.where(lower, 0.0, turned).astype(BF16)
        return carry

    lax.fori_loop(0, TILE, step, 0, unroll=4)


def gradient(left, cots, grads, e, slot):
    rows = left[...]
    for m in range(MATS):
        halves = []
        for col in range(0, COLS, 2):
            right = jnp.concatenate([cots[e, col, m], cots[e, col + 1, m]], axis=1)
            halves.append(dot(rows, right).reshape(TILE, ROWS, 2 * TILE))
        at = (slot * MATS + m) * 2 * ROWS
        grads[:, at : at + 2 * ROWS, :] = jnp.concatenate(halves, axis=1).astype(BF16)


def project(grads, weights, quads):
    def step(two, carry):
        outs = [dot(grads[two * 2 + u], weights[two * 2 + u]) for u in range(2)]
        at = pl.multiple_of(two * 2 * ROWS, 2 * ROWS)
        for slot in range(BATCH):
            for pair in range(PAIRS):
                src = (slot * PAIRS + pair) * ROWS
                both = jnp.concatenate([out[src : src + ROWS] for out in outs], axis=0)
                quads[slot, pl.ds(at, 2 * ROWS), pair * TILE : (pair + 1) * TILE] = both.astype(BF16)
        return carry

    lax.fori_loop(0, TILE // 2, step, 0, unroll=16)


def select(quads, count, picked, slot, kind):
    row_in_group = lax.rem(lax.broadcasted_iota(jnp.int32, (TILE * ROWS, TILE), 0), ROWS)
    lane_group = lax.broadcasted_iota(jnp.int32, (TILE * ROWS, TILE), 1) // BLOCKS
    sums = dot(quads[slot], count[kind])
    folded = jnp.where(row_in_group >= 4, sums[:, TILE:], sums[:, :TILE])
    picked[...] = jnp.where(lane_group == lax.rem(row_in_group, 4), folded, 0.0)
    total = picked[pl.ds(0, TILE, stride=ROWS), :]
    for i in range(1, ROWS):
        total += picked[pl.ds(i, TILE, stride=ROWS), :]
    turned = total.T
    return turned[0:32] + turned[32:64] + turned[64:96] + turned[96:128]


def kernel(
    in_hbm, cot_hbm, bank_hbm, tiles_hbm, blocks_hbm, signs_hbm, test_hbm, out_ref,
    bank, bank_t, weights, hits, cots, ins, left32, left, grads, quads, picked, count, tests,
    raw, sums_out, sums_in, done,
    load_sem, own_sem, j_send, j_recv, i_send, i_recv, p_send, p_recv, t_send, t_recv, ex_send, ex_recv,
):
    me = lax.axis_index("param")
    mx = lax.axis_index("ex")
    core = lax.rem(me, 2)
    y = lax.rem(me // 2, 4)
    z = me // 8

    def device(zz, yy, cc):
        return (zz * 4 + yy) * 2 + cc

    def along_y(distance):
        return device(z, lax.rem(y + distance, 4), core)

    def along_z(distance):
        return device(lax.rem(z + distance, 4), y, core)

    sibling = device(z, y, 1 - core)
    family, member = me // 4, lax.rem(me, 4)
    alone = member == mx

    barrier = pltpu.get_barrier_semaphore()

    def greet(**to):
        pl.semaphore_signal(barrier, inc=1, device_id=to, device_id_type=MESH)

    for d in (1, 3, 2):
        greet(param=along_y(d))
        greet(param=along_z(d))
    greet(param=sibling)
    for j in range(4):
        sender = family * 4 + j

        @pl.when(jnp.logical_or(sender != me, member != mx))
        def _(sender=sender):
            greet(param=sender, ex=member)

    loads = [
        pltpu.make_async_copy(tiles_hbm, hits.at[0], load_sem.at[0]),
        pltpu.make_async_copy(blocks_hbm, hits.at[1], load_sem.at[1]),
        pltpu.make_async_copy(signs_hbm, hits.at[2], load_sem.at[2]),
        pltpu.make_async_copy(bank_hbm, bank, load_sem.at[3]),
    ]
    for copy in loads:
        copy.start()
    own = []
    for kind in range(2):
        pair = pl.ds(2 * kind, 2)
        col_pos, row_pos = (y, z) if kind == 0 else (z, y)
        own.append(
            pltpu.make_async_copy(
                in_hbm.at[pair], ins.at[pair, row_pos * 2 + core], own_sem.at[kind]
            )
        )
        for e in (2 * kind, 2 * kind + 1):
            own.append(
                pltpu.make_async_copy(cot_hbm.at[:, e], cots.at[e, col_pos], own_sem.at[2 + e])
            )
    for copy in own:
        copy.start()

    for copy in loads[:3]:
        copy.wait()
    count_hits(hits, count, z, y, core)
    loads[3].wait()
    turn_bank(bank, bank_t)
    pl.semaphore_wait(barrier, 7 + jnp.where(alone, 3, 4))

    def send(src, dst, send_sem, recv_sem, **to):
        copy = pltpu.make_async_remote_copy(
            src_ref=src, dst_ref=dst, send_sem=send_sem, recv_sem=recv_sem, device_id=to, device_id_type=MESH
        )
        copy.start()
        return copy

    cols, rows, relays = {}, {}, {}

    def rings(e):
        return ((y, along_y), (z, along_z)) if e < 2 else ((z, along_z), (y, along_y))

    def send_tiles(batch):
        for e in batch:
            pos, to = rings(e)[1]
            place = ins.at[e, pos * 2 + core]
            for d in (2, 1, 3):
                rows[e, d] = send(in_hbm.at[e], place, i_send.at[e, d], i_recv.at[e, d], param=to(d))
            relays[e, 0] = send(in_hbm.at[e], place, p_send.at[e, 0], p_recv.at[e, 0], param=sibling)
        for e in batch:
            pos, to = rings(e)[0]
            for d in (2, 1, 3):
                cols[e, d] = send(
                    cot_hbm.at[:, e], cots.at[e, pos], j_send.at[e, d], j_recv.at[e, d], param=to(d)
                )

    def relay_rows(batch):
        for e in batch:
            pos = rings(e)[1][0]
            for d in (1, 3, 2):
                rows[e, d].wait_recv()
                place = ins.at[e, lax.rem(pos + 4 - d, 4) * 2 + core]
                relays[e, d] = send(place, place, p_send.at[e, d], p_recv.at[e, d], param=sibling)

    def gradients(batch):
        for slot, e in enumerate(batch):
            for index in range(4):
                relays[e, index].wait_recv()
            turn_rows(ins, left32, left, e)
            for d in (1, 3, 2):
                cols[e, d].wait_recv()
            gradient(left, cots, grads, e, slot)

    def finish(batch):
        project(grads, weights, quads)
        for slot, e in enumerate(batch):
            raw[pl.ds(e, BLOCKS, stride=EX), :] = select(quads, count, picked, slot, e // 2)

    early, late = ORDER[:BATCH], ORDER[BATCH:]
    send_tiles(early)
    spread_bank(bank_t, weights)
    for copy in own:
        copy.wait()
    relay_rows(early)
    send_tiles(late)
    tests_out = [
        send(
            test_hbm, tests.at[member], t_send.at[d], t_recv.at[member],
            param=family * 4 + mx, ex=lax.rem(mx + d, 4),
        )
        for d in range(1, 4)
    ]
    test_here = pltpu.make_async_copy(test_hbm, tests.at[member], t_recv.at[member])
    test_near = pltpu.make_async_remote_copy(
        src_ref=test_hbm,
        dst_ref=tests.at[member],
        send_sem=t_send.at[0],
        recv_sem=t_recv.at[member],
        device_id={"param": family * 4 + mx, "ex": mx},
        device_id_type=MESH,
    )

    @pl.when(alone)
    def _():
        test_here.start()

    @pl.when(jnp.logical_not(alone))
    def _():
        test_near.start()

    gradients(early)
    relay_rows(late)
    finish(early)
    gradients(late)
    finish(late)
    sums_out[...] = raw[...].astype(BF16).reshape(8, 4 * EX, TILE)

    others = sorted(
        [(dz, dy, dc) for dz in range(4) for dy in range(4) for dc in range(2)][1:],
        key=lambda d: -(min(d[0], 4 - d[0]) + min(d[1], 4 - d[1])),
    )

    def exchange(index, source, incoming, beside=None):
        for dz, dy, dc in others:
            to = device(lax.rem(z + dz, 4), lax.rem(y + dy, 4), lax.rem(core + dc, 2))
            send(source(to), incoming.at[me], ex_send.at[index], ex_recv.at[index], param=to)
        if beside is not None:
            beside()
        rest = incoming.at[pl.ds(0, GROUP - 1)]
        pltpu.make_async_copy(rest, rest, ex_recv.at[index]).wait()
        return pltpu.make_async_copy(rest, rest, ex_send.at[index])

    def drain():
        for j in range(4):
            pltpu.make_async_copy(tests.at[j], tests.at[j], t_recv.at[j]).wait()
        for copy in [*cols.values(), *rows.values(), *relays.values(), *tests_out]:
            copy.wait_send()

        @pl.when(jnp.logical_not(alone))
        def _():
            test_near.wait_send()

    sums_in[me] = sums_out[family]
    sums_sent = exchange(0, lambda to: sums_out.at[to // 4], sums_in, drain)
    features = jnp.sum(sums_in[...].astype(F32), axis=0) * SCALE
    high = features.astype(BF16)
    low = (features - high.astype(F32)).astype(BF16)
    scores = jnp.zeros((2 * EX, 256), F32)
    for j in range(4):
        both = jnp.concatenate([high[j * EX : (j + 1) * EX], low[j * EX : (j + 1) * EX]], axis=0)
        scores += dot_nt(both, tests[j])
    done[me] = scores[:EX] + scores[EX:]
    scores_sent = exchange(1, lambda to: done.at[me], done, sums_sent.wait)
    for j in range(4):
        total = done[j]
        for other in range(1, 8):
            total += done[other * 4 + j]
        out_ref[:, j * 256 : (j + 1) * 256] = total
    scores_sent.wait()


def local(inputs, cotangents, jl_bank, jl_tiles, jl_blocks, jl_signs, test_features):
    turned = [jnp.transpose(a, (0, 1, 3, 2)) for a in (jl_tiles, jl_blocks, jl_signs)]
    anywhere = pl.BlockSpec(memory_space=pl.ANY)
    dma = pltpu.SemaphoreType.DMA
    return pl.pallas_call(
        kernel,
        out_shape=jax.ShapeDtypeStruct((EX, 1024), F32),
        in_specs=[anywhere] * 7,
        out_specs=pl.BlockSpec(memory_space=pltpu.VMEM),
        scratch_shapes=[
            pltpu.VMEM((BANK, TILE, TILE), BF16),
            pltpu.VMEM((TILE * BANK, TILE), F32),
            pltpu.VMEM((TILE, 2 * TILE, 2 * BANK), BF16),
            pltpu.VMEM((3, MATS, GROUP, HITS, GROUP), jnp.int32),
            pltpu.VMEM((EX, COLS, MATS, TOK, TILE), BF16),
            pltpu.VMEM((EX, ROWS, TOK, TILE), BF16),
            pltpu.VMEM((TILE * ROWS, TOK), F32),
            pltpu.VMEM((TILE * ROWS, TOK), BF16),
            pltpu.VMEM((TILE, BATCH * PAIRS * ROWS, 2 * TILE), BF16),
            pltpu.VMEM((BATCH, TILE * ROWS, PAIRS * TILE), BF16),
            pltpu.VMEM((TILE * ROWS, TILE), F32),
            pltpu.VMEM((2, MATS * COLS * BANK, 2 * TILE), BF16),
            pltpu.VMEM((4, 256, TILE), BF16),
            pltpu.VMEM((BLOCKS * EX, TILE), F32),
            pltpu.VMEM((8, 4 * EX, TILE), BF16),
            pltpu.VMEM((GROUP, 4 * EX, TILE), BF16),
            pltpu.VMEM((GROUP, EX, 256), F32),
            dma((4,)),
            dma((2 + EX,)),
            dma((EX, 4)),
            dma((EX, 4)),
            dma((EX, 4)),
            dma((EX, 4)),
            dma((EX, 4)),
            dma((EX, 4)),
            dma((4,)),
            dma((4,)),
            dma((2,)),
            dma((2,)),
        ],
        compiler_params=pltpu.CompilerParams(
            collective_id=0, has_side_effects=True, vmem_limit_bytes=56 * 1024 * 1024
        ),
        cost_estimate=pl.CostEstimate(flops=9_000_000_000, bytes_accessed=8_000_000, transcendentals=0),
    )(inputs, cotangents, jl_bank, *turned, test_features)


def solution(mesh):
    placed = (
        P("ex", None, "param"),
        P(None, "ex", None, "param"),
        P(),
        P(),
        P(),
        P(),
        P("ex", "param"),
    )
    return jax.shard_map(
        local, mesh=mesh, in_specs=placed, out_specs=P("ex", None), check_vma=False
    )
```

time: 49.9 us -> 45.7 us (0.916)
  Pallas kernels: 48.4 us -> 44.2 us
    pallas_call x1, Pallas kernels: 48.4 us -> 44.2 us  [local(): pl.pallas_call(kernel, out_shape=jax.ShapeDtypeStruct((EX, 1024), F32), i...]
where the time goes in v4:
time: 45.7 us; the launch traced here: 45.5 us
  Pallas kernels  44.2 us (97%)
  local copies, waits for them, and re-layouts  1.32 us (3%)
    pallas_call x1, Pallas kernels, local(): pl.pallas_call(kernel, out_shape=jax.ShapeDtypeStruct((EX, 1024), F32), i...  44.2 us
    unnamed x1, local copies, waits for them, and re-layouts  1.32 us

profile of v4, /device:TPU:1, one launch (start us, length us, event | category | flops | bytes accessed | tf_op | source)
XLA Modules:
  0.0 45.5 jit_solution(1275011815222676246)
XLA Ops:
  0.0 44.2 %shard_map.73 = f32[4,1024]{1,0:T(4,128)} custom-call(bf16[4,128,128]{2,1,0:T(8,128)(2,1)} %in_hbm.1, bf16[3,4,128,128]{3,2,1,0:T(8,128)(2,1)} %cot_hbm.1, bf16[64,128,128]{2,1,0:T(8,128)(2,1)} %bank_hbm.1, s32[3,32,8,32]{3,2,1,0:T(8,128)} %bitcast.3, s32[3,32,8,32]{3,2,1,0:T(8,128)} %bitcast.4, s32[3,32,8,32]{3,2,1,0:T(8,128)} %bitcast.5, ...), custom_call_target="tpu_custom_call" | custom-call | flops 8999999488 | bytes 8000000 | tf_op jit(solution)/shard_map/pallas_call | solution.py:364
  44.2 1.3 %copy.9 = f32[4,1024]{1,0:T(4,128)} copy(f32[4,1024]{1,0:T(4,128)} %shard_map.73) | data formatting | bytes 32768

commit v5 on v4

--- a/solution.py
+++ b/solution.py
@@ -22,6 +22,7 @@
 PAIRS = MATS * COLS // 2
 GROUP = 32
 BATCH = 2
+UNROLL = 32
 MESH = pl.DeviceIdType.MESH
 F32 = jnp.float32
 BF16 = jnp.bfloat16
@@ -31,10 +32,6 @@
 
 def dot(a, b):
     return lax.dot_general(a, b, (((1,), (0,)), ((), ())), preferred_element_type=F32)
-
-
-def dot_nt(a, b):
-    return lax.dot_general(a, b, (((1,), (1,)), ((), ())), preferred_element_type=F32)
 
 
 def count_hits(hits, count, z, y, core):
@@ -94,13 +91,10 @@
     lax.fori_loop(0, BANK, turn, 0, unroll=4)
 
 
-def turn_rows(ins, left32, left, e):
-    def turn(i, carry):
-        left32[pl.ds(i, TILE, stride=ROWS), :] = ins[e, i].astype(F32).T
-        return carry
-
-    lax.fori_loop(0, ROWS, turn, 0, unroll=4)
-    left[...] = left32[...].astype(BF16)
+def turn_rows(ins, left32, left, e, slot):
+    for i in range(ROWS):
+        left32[slot, pl.ds(i, TILE, stride=ROWS), :] = ins[e, i].astype(F32).T
+    left[slot] = left32[slot].astype(BF16)
 
 
 def spread_bank(bank_t, weights):
@@ -117,7 +111,7 @@
 
 
 def gradient(left, cots, grads, e, slot):
-    rows = left[...]
+    rows = left[slot]
     for m in range(MATS):
         halves = []
         for col in range(0, COLS, 2):
@@ -138,7 +132,7 @@
                 quads[slot, pl.ds(at, 2 * ROWS), pair * TILE : (pair + 1) * TILE] = both.astype(BF16)
         return carry
 
-    lax.fori_loop(0, TILE // 2, step, 0, unroll=16)
+    lax.fori_loop(0, TILE // 2, step, 0, unroll=UNROLL)
 
 
 def select(quads, count, picked, slot, kind):
@@ -146,17 +140,17 @@
     lane_group = lax.broadcasted_iota(jnp.int32, (TILE * ROWS, TILE), 1) // BLOCKS
     sums = dot(quads[slot], count[kind])
     folded = jnp.where(row_in_group >= 4, sums[:, TILE:], sums[:, :TILE])
-    picked[...] = jnp.where(lane_group == lax.rem(row_in_group, 4), folded, 0.0)
-    total = picked[pl.ds(0, TILE, stride=ROWS), :]
+    picked[slot] = jnp.where(lane_group == lax.rem(row_in_group, 4), folded, 0.0)
+    total = picked[slot, pl.ds(0, TILE, stride=ROWS), :]
     for i in range(1, ROWS):
-        total += picked[pl.ds(i, TILE, stride=ROWS), :]
+        total += picked[slot, pl.ds(i, TILE, stride=ROWS), :]
     turned = total.T
     return turned[0:32] + turned[32:64] + turned[64:96] + turned[96:128]
 
 
 def kernel(
     in_hbm, cot_hbm, bank_hbm, tiles_hbm, blocks_hbm, signs_hbm, test_hbm, out_ref,
-    bank, bank_t, weights, hits, cots, ins, left32, left, grads, quads, picked, count, tests,
+    bank, bank_t, weights, hits, cots, ins, left32, left, grads, quads, picked, count, tests, tests_t,
     raw, sums_out, sums_in, done,
     load_sem, own_sem, j_send, j_recv, i_send, i_recv, p_send, p_recv, t_send, t_recv, ex_send, ex_recv,
 ):
@@ -222,8 +216,6 @@
     for copy in loads[:3]:
         copy.wait()
     count_hits(hits, count, z, y, core)
-    loads[3].wait()
-    turn_bank(bank, bank_t)
     pl.semaphore_wait(barrier, 7 + jnp.where(alone, 3, 4))
 
     def send(src, dst, send_sem, recv_sem, **to):
@@ -264,9 +256,11 @@
         for slot, e in enumerate(batch):
             for index in range(4):
                 relays[e, index].wait_recv()
-            turn_rows(ins, left32, left, e)
+            turn_rows(ins, left32, left, e, slot)
+        for slot, e in enumerate(batch):
             for d in (1, 3, 2):
                 cols[e, d].wait_recv()
+        for slot, e in enumerate(batch):
             gradient(left, cots, grads, e, slot)
 
     def finish(batch):
@@ -276,6 +270,8 @@
 
     early, late = ORDER[:BATCH], ORDER[BATCH:]
     send_tiles(early)
+    loads[3].wait()
+    turn_bank(bank, bank_t)
     spread_bank(bank_t, weights)
     for copy in own:
         copy.wait()
@@ -331,6 +327,9 @@
     def drain():
         for j in range(4):
             pltpu.make_async_copy(tests.at[j], tests.at[j], t_recv.at[j]).wait()
+            for half in range(2):
+                piece = tests[j, half * TILE : (half + 1) * TILE].astype(F32).T
+                tests_t[j, :, half * TILE : (half + 1) * TILE] = piece.astype(BF16)
         for copy in [*cols.values(), *rows.values(), *relays.values(), *tests_out]:
             copy.wait_send()
 
@@ -346,7 +345,7 @@
     scores = jnp.zeros((2 * EX, 256), F32)
     for j in range(4):
         both = jnp.concatenate([high[j * EX : (j + 1) * EX], low[j * EX : (j + 1) * EX]], axis=0)
-        scores += dot_nt(both, tests[j])
+        scores += dot(both, tests_t[j])
     done[me] = scores[:EX] + scores[EX:]
     scores_sent = exchange(1, lambda to: done.at[me], done, sums_sent.wait)
     for j in range(4):
@@ -373,13 +372,14 @@
             pltpu.VMEM((3, MATS, GROUP, HITS, GROUP), jnp.int32),
             pltpu.VMEM((EX, COLS, MATS, TOK, TILE), BF16),
             pltpu.VMEM((EX, ROWS, TOK, TILE), BF16),
-            pltpu.VMEM((TILE * ROWS, TOK), F32),
-            pltpu.VMEM((TILE * ROWS, TOK), BF16),
+            pltpu.VMEM((BATCH, TILE * ROWS, TOK), F32),
+            pltpu.VMEM((BATCH, TILE * ROWS, TOK), BF16),
             pltpu.VMEM((TILE, BATCH * PAIRS * ROWS, 2 * TILE), BF16),
             pltpu.VMEM((BATCH, TILE * ROWS, PAIRS * TILE), BF16),
-            pltpu.VMEM((TILE * ROWS, TILE), F32),
+            pltpu.VMEM((BATCH, TILE * ROWS, TILE), F32),
             pltpu.VMEM((2, MATS * COLS * BANK, 2 * TILE), BF16),
             pltpu.VMEM((4, 256, TILE), BF16),
+            pltpu.VMEM((4, TILE, 256), BF16),
             pltpu.VMEM((BLOCKS * EX, TILE), F32),
             pltpu.VMEM((8, 4 * EX, TILE), BF16),
             pltpu.VMEM((GROUP, 4 * EX, TILE), BF16),

time: 45.7 us -> 42.2 us (0.923)
  Pallas kernels: 44.2 us -> 40.7 us
    pallas_call x1, Pallas kernels: 44.2 us -> 40.7 us  [local(): pl.pallas_call(kernel, out_shape=jax.ShapeDtypeStruct((EX, 1024), F32), i...]
where the time goes in v5:
time: 42.2 us; the launch traced here: 42 us
  Pallas kernels  40.7 us (96%)
  local copies, waits for them, and re-layouts  1.32 us (3%)
    pallas_call x1, Pallas kernels, local(): pl.pallas_call(kernel, out_shape=jax.ShapeDtypeStruct((EX, 1024), F32), i...  40.7 us
    unnamed x1, local copies, waits for them, and re-layouts  1.32 us

profile of v5, /device:TPU:1, one launch (start us, length us, event | category | flops | bytes accessed | tf_op | source)
XLA Modules:
  0.0 42.0 jit_solution(2331091138757763786)
XLA Ops:
  0.0 40.7 %shard_map.73 = f32[4,1024]{1,0:T(4,128)} custom-call(bf16[4,128,128]{2,1,0:T(8,128)(2,1)} %in_hbm.1, bf16[3,4,128,128]{3,2,1,0:T(8,128)(2,1)} %cot_hbm.1, bf16[64,128,128]{2,1,0:T(8,128)(2,1)} %bank_hbm.1, s32[3,32,8,32]{3,2,1,0:T(8,128)} %bitcast.3, s32[3,32,8,32]{3,2,1,0:T(8,128)} %bitcast.4, s32[3,32,8,32]{3,2,1,0:T(8,128)} %bitcast.5, ...), custom_call_target="tpu_custom_call" | custom-call | flops 8999999488 | bytes 8000000 | tf_op jit(solution)/shard_map/pallas_call | solution.py:363
  40.7 1.3 %copy.9 = f32[4,1024]{1,0:T(4,128)} copy(f32[4,1024]{1,0:T(4,128)} %shard_map.73) | data formatting | bytes 32768

commit v6 on v5

--- a/solution.py
+++ b/solution.py
@@ -226,6 +226,7 @@
         return copy
 
     cols, rows, relays = {}, {}, {}
+    early, late = ORDER[:BATCH], ORDER[BATCH:]
 
     def rings(e):
         return ((y, along_y), (z, along_z)) if e < 2 else ((z, along_z), (y, along_y))
@@ -252,38 +253,7 @@
                 place = ins.at[e, lax.rem(pos + 4 - d, 4) * 2 + core]
                 relays[e, d] = send(place, place, p_send.at[e, d], p_recv.at[e, d], param=sibling)
 
-    def gradients(batch):
-        for slot, e in enumerate(batch):
-            for index in range(4):
-                relays[e, index].wait_recv()
-            turn_rows(ins, left32, left, e, slot)
-        for slot, e in enumerate(batch):
-            for d in (1, 3, 2):
-                cols[e, d].wait_recv()
-        for slot, e in enumerate(batch):
-            gradient(left, cots, grads, e, slot)
-
-    def finish(batch):
-        project(grads, weights, quads)
-        for slot, e in enumerate(batch):
-            raw[pl.ds(e, BLOCKS, stride=EX), :] = select(quads, count, picked, slot, e // 2)
-
-    early, late = ORDER[:BATCH], ORDER[BATCH:]
-    send_tiles(early)
-    loads[3].wait()
-    turn_bank(bank, bank_t)
-    spread_bank(bank_t, weights)
-    for copy in own:
-        copy.wait()
-    relay_rows(early)
-    send_tiles(late)
-    tests_out = [
-        send(
-            test_hbm, tests.at[member], t_send.at[d], t_recv.at[member],
-            param=family * 4 + mx, ex=lax.rem(mx + d, 4),
-        )
-        for d in range(1, 4)
-    ]
+    tests_out = []
     test_here = pltpu.make_async_copy(test_hbm, tests.at[member], t_recv.at[member])
     test_near = pltpu.make_async_remote_copy(
         src_ref=test_hbm,
@@ -294,14 +264,49 @@
         device_id_type=MESH,
     )
 
-    @pl.when(alone)
-    def _():
-        test_here.start()
-
-    @pl.when(jnp.logical_not(alone))
-    def _():
-        test_near.start()
-
+    def send_tests():
+        for d in range(1, 4):
+            tests_out.append(
+                send(
+                    test_hbm, tests.at[member], t_send.at[d], t_recv.at[member],
+                    param=family * 4 + mx, ex=lax.rem(mx + d, 4),
+                )
+            )
+
+        @pl.when(alone)
+        def _():
+            test_here.start()
+
+        @pl.when(jnp.logical_not(alone))
+        def _():
+            test_near.start()
+
+    def gradients(batch):
+        for slot, e in enumerate(batch):
+            for index in range(4):
+                relays[e, index].wait_recv()
+            turn_rows(ins, left32, left, e, slot)
+        for slot, e in enumerate(batch):
+            for d in (1, 3, 2):
+                cols[e, d].wait_recv()
+        if batch == late:
+            send_tests()
+        for slot, e in enumerate(batch):
+            gradient(left, cots, grads, e, slot)
+
+    def finish(batch):
+        project(grads, weights, quads)
+        for slot, e in enumerate(batch):
+            raw[pl.ds(e, BLOCKS, stride=EX), :] = select(quads, count, picked, slot, e // 2)
+
+    send_tiles(early)
+    loads[3].wait()
+    turn_bank(bank, bank_t)
+    spread_bank(bank_t, weights)
+    for copy in own:
+        copy.wait()
+    relay_rows(early)
+    send_tiles(late)
     gradients(early)
     relay_rows(late)
     finish(early)

time: 42.2 us -> 41.8 us (level)
  no operation moved by 1% of the time
where the time goes in v6:
time: 41.8 us; the launch traced here: 41.7 us
  Pallas kernels  40.3 us (96%)
  local copies, waits for them, and re-layouts  1.32 us (3%)
    pallas_call x1, Pallas kernels, local(): pl.pallas_call(kernel, out_shape=jax.ShapeDtypeStruct((EX, 1024), F32), i...  40.3 us
    unnamed x1, local copies, waits for them, and re-layouts  1.32 us

profile of v6, /device:TPU:1, one launch (start us, length us, event | category | flops | bytes accessed | tf_op | source)
XLA Modules:
  0.0 41.7 jit_solution(14247600649937273463)
XLA Ops:
  0.0 40.3 %shard_map.73 = f32[4,1024]{1,0:T(4,128)} custom-call(bf16[4,128,128]{2,1,0:T(8,128)(2,1)} %in_hbm.1, bf16[3,4,128,128]{3,2,1,0:T(8,128)(2,1)} %cot_hbm.1, bf16[64,128,128]{2,1,0:T(8,128)(2,1)} %bank_hbm.1, s32[3,32,8,32]{3,2,1,0:T(8,128)} %bitcast.3, s32[3,32,8,32]{3,2,1,0:T(8,128)} %bitcast.4, s32[3,32,8,32]{3,2,1,0:T(8,128)} %bitcast.5, ...), custom_call_target="tpu_custom_call" | custom-call | flops 8999999488 | bytes 8000000 | tf_op jit(solution)/shard_map/pallas_call | solution.py:368
  40.3 1.3 %copy.9 = f32[4,1024]{1,0:T(4,128)} copy(f32[4,1024]{1,0:T(4,128)} %shard_map.73) | data formatting | bytes 32768

commit v7 on v6

--- a/solution.py
+++ b/solution.py
@@ -178,17 +178,17 @@
     def greet(**to):
         pl.semaphore_signal(barrier, inc=1, device_id=to, device_id_type=MESH)
 
-    for d in (1, 3, 2):
+    for j in range(4):
+        sender = family * 4 + j
+
+        @pl.when(jnp.logical_or(sender != me, member != mx))
+        def _(sender=sender):
+            greet(param=sender, ex=member)
+
+    for d in (2, 1, 3):
         greet(param=along_y(d))
         greet(param=along_z(d))
     greet(param=sibling)
-    for j in range(4):
-        sender = family * 4 + j
-
-        @pl.when(jnp.logical_or(sender != me, member != mx))
-        def _(sender=sender):
-            greet(param=sender, ex=member)
-
     loads = [
         pltpu.make_async_copy(tiles_hbm, hits.at[0], load_sem.at[0]),
         pltpu.make_async_copy(blocks_hbm, hits.at[1], load_sem.at[1]),
@@ -213,9 +213,6 @@
     for copy in own:
         copy.start()
 
-    for copy in loads[:3]:
-        copy.wait()
-    count_hits(hits, count, z, y, core)
     pl.semaphore_wait(barrier, 7 + jnp.where(alone, 3, 4))
 
     def send(src, dst, send_sem, recv_sem, **to):
@@ -300,13 +297,17 @@
             raw[pl.ds(e, BLOCKS, stride=EX), :] = select(quads, count, picked, slot, e // 2)
 
     send_tiles(early)
+
+    for copy in loads[:3]:
+        copy.wait()
+    count_hits(hits, count, z, y, core)
     loads[3].wait()
     turn_bank(bank, bank_t)
-    spread_bank(bank_t, weights)
     for copy in own:
         copy.wait()
     relay_rows(early)
     send_tiles(late)
+    spread_bank(bank_t, weights)
     gradients(early)
     relay_rows(late)
     finish(early)

time: 41.8 us -> 40.7 us (0.974)
  Pallas kernels: 40.3 us -> 39.2 us
    pallas_call x1, Pallas kernels: 40.3 us -> 39.2 us  [local(): pl.pallas_call(kernel, out_shape=jax.ShapeDtypeStruct((EX, 1024), F32), i...]
where the time goes in v7:
time: 40.7 us; the launch traced here: 40.5 us
  Pallas kernels  39.2 us (96%)
  local copies, waits for them, and re-layouts  1.32 us (3%)
    pallas_call x1, Pallas kernels, local(): pl.pallas_call(kernel, out_shape=jax.ShapeDtypeStruct((EX, 1024), F32), i...  39.2 us
    unnamed x1, local copies, waits for them, and re-layouts  1.32 us

profile of v7, /device:TPU:1, one launch (start us, length us, event | category | flops | bytes accessed | tf_op | source)
XLA Modules:
  0.0 40.5 jit_solution(16411529858109771715)
XLA Ops:
  0.0 39.2 %shard_map.73 = f32[4,1024]{1,0:T(4,128)} custom-call(bf16[4,128,128]{2,1,0:T(8,128)(2,1)} %in_hbm.1, bf16[3,4,128,128]{3,2,1,0:T(8,128)(2,1)} %cot_hbm.1, bf16[64,128,128]{2,1,0:T(8,128)(2,1)} %bank_hbm.1, s32[3,32,8,32]{3,2,1,0:T(8,128)} %bitcast.3, s32[3,32,8,32]{3,2,1,0:T(8,128)} %bitcast.4, s32[3,32,8,32]{3,2,1,0:T(8,128)} %bitcast.5, ...), custom_call_target="tpu_custom_call" | custom-call | flops 8999999488 | bytes 8000000 | tf_op jit(solution)/shard_map/pallas_call | solution.py:369
  39.2 1.3 %copy.9 = f32[4,1024]{1,0:T(4,128)} copy(f32[4,1024]{1,0:T(4,128)} %shard_map.73) | data formatting | bytes 32768

commit v8 on v7

--- a/solution.py
+++ b/solution.py
@@ -22,7 +22,7 @@
 PAIRS = MATS * COLS // 2
 GROUP = 32
 BATCH = 2
-UNROLL = 32
+UNROLL = 64
 MESH = pl.DeviceIdType.MESH
 F32 = jnp.float32
 BF16 = jnp.bfloat16
@@ -88,7 +88,7 @@
         bank_t[pl.ds(r, TILE, stride=BANK), :] = bank[r].astype(F32).T
         return carry
 
-    lax.fori_loop(0, BANK, turn, 0, unroll=4)
+    lax.fori_loop(0, BANK, turn, 0, unroll=16)
 
 
 def turn_rows(ins, left32, left, e, slot):
@@ -107,7 +107,7 @@
         weights[a, TILE:] = jnp.where(lower, 0.0, turned).astype(BF16)
         return carry
 
-    lax.fori_loop(0, TILE, step, 0, unroll=4)
+    lax.fori_loop(0, TILE, step, 0, unroll=16)
 
 
 def gradient(left, cots, grads, e, slot):

time: 40.7 us -> 39.9 us (0.980)
  Pallas kernels: 39.2 us -> 38.4 us
    pallas_call x1, Pallas kernels: 39.2 us -> 38.4 us  [local(): pl.pallas_call(kernel, out_shape=jax.ShapeDtypeStruct((EX, 1024), F32), i...]
where the time goes in v8:
time: 39.9 us; the launch traced here: 39.8 us
  Pallas kernels  38.4 us (96%)
  local copies, waits for them, and re-layouts  1.32 us (3%)
    pallas_call x1, Pallas kernels, local(): pl.pallas_call(kernel, out_shape=jax.ShapeDtypeStruct((EX, 1024), F32), i...  38.4 us
    unnamed x1, local copies, waits for them, and re-layouts  1.32 us

profile of v8, /device:TPU:1, one launch (start us, length us, event | category | flops | bytes accessed | tf_op | source)
XLA Modules:
  0.0 39.8 jit_solution(6138215778601660490)
XLA Ops:
  0.0 38.4 %shard_map.73 = f32[4,1024]{1,0:T(4,128)} custom-call(bf16[4,128,128]{2,1,0:T(8,128)(2,1)} %in_hbm.1, bf16[3,4,128,128]{3,2,1,0:T(8,128)(2,1)} %cot_hbm.1, bf16[64,128,128]{2,1,0:T(8,128)(2,1)} %bank_hbm.1, s32[3,32,8,32]{3,2,1,0:T(8,128)} %bitcast.3, s32[3,32,8,32]{3,2,1,0:T(8,128)} %bitcast.4, s32[3,32,8,32]{3,2,1,0:T(8,128)} %bitcast.5, ...), custom_call_target="tpu_custom_call" | custom-call | flops 8999999488 | bytes 8000000 | tf_op jit(solution)/shard_map/pallas_call | solution.py:369
  38.4 1.3 %copy.9 = f32[4,1024]{1,0:T(4,128)} copy(f32[4,1024]{1,0:T(4,128)} %shard_map.73) | data formatting | bytes 32768

commit v9 on v8

--- a/solution.py
+++ b/solution.py
@@ -88,7 +88,7 @@
         bank_t[pl.ds(r, TILE, stride=BANK), :] = bank[r].astype(F32).T
         return carry
 
-    lax.fori_loop(0, BANK, turn, 0, unroll=16)
+    lax.fori_loop(0, BANK, turn, 0, unroll=32)
 
 
 def turn_rows(ins, left32, left, e, slot):
@@ -107,7 +107,7 @@
         weights[a, TILE:] = jnp.where(lower, 0.0, turned).astype(BF16)
         return carry
 
-    lax.fori_loop(0, TILE, step, 0, unroll=16)
+    lax.fori_loop(0, TILE, step, 0, unroll=32)
 
 
 def gradient(left, cots, grads, e, slot):

time: 39.9 us -> 39.9 us (level)
  no operation moved by 1% of the time
where the time goes in v9:
time: 39.9 us; the launch traced here: 39.8 us
  Pallas kernels  38.4 us (96%)
  local copies, waits for them, and re-layouts  1.32 us (3%)
    pallas_call x1, Pallas kernels, local(): pl.pallas_call(kernel, out_shape=jax.ShapeDtypeStruct((EX, 1024), F32), i...  38.4 us
    unnamed x1, local copies, waits for them, and re-layouts  1.32 us

profile of v9, /device:TPU:1, one launch (start us, length us, event | category | flops | bytes accessed | tf_op | source)
XLA Modules:
  0.0 39.8 jit_solution(6797065122747232730)
XLA Ops:
  0.0 38.4 %shard_map.73 = f32[4,1024]{1,0:T(4,128)} custom-call(bf16[4,128,128]{2,1,0:T(8,128)(2,1)} %in_hbm.1, bf16[3,4,128,128]{3,2,1,0:T(8,128)(2,1)} %cot_hbm.1, bf16[64,128,128]{2,1,0:T(8,128)(2,1)} %bank_hbm.1, s32[3,32,8,32]{3,2,1,0:T(8,128)} %bitcast.3, s32[3,32,8,32]{3,2,1,0:T(8,128)} %bitcast.4, s32[3,32,8,32]{3,2,1,0:T(8,128)} %bitcast.5, ...), custom_call_target="tpu_custom_call" | custom-call | flops 8999999488 | bytes 8000000 | tf_op jit(solution)/shard_map/pallas_call | solution.py:369
  38.4 1.3 %copy.9 = f32[4,1024]{1,0:T(4,128)} copy(f32[4,1024]{1,0:T(4,128)} %shard_map.73) | data formatting | bytes 32768
